TPU v7x, 128 devices: a whole 4x4x4 slice. The times are simulated.
128 devices in a mesh: dp: 8 (over y_hi, x), ha: 4 (over z), wa: 4 (over y_lo, core).
Axes of the slice: x: 4, y: 4 (y_hi: 2, y_lo: 2; y = y_hi * 2 + y_lo), z: 4, core: 2. Of those that a mesh axis runs over, the one named last changes fastest.
Arguments:
- query_in: bfloat16 [8, 4, 4, 384, 512], P('dp', 'ha', 'wa'), may hold values from -30 to 30
- key_in: bfloat16 [8, 4, 4, 384, 512], P('dp', 'ha', 'wa'), may hold values from -6 to 6
- value_in: bfloat16 [8, 4, 4, 384, 512], P('dp', 'ha', 'wa'), may hold values from -6 to 6
- grad_out: bfloat16 [8, 4, 4, 384, 3072], P('dp', 'ha', 'wa'), may hold values from -1.5 to 1.5
- out_weight: bfloat16 [512, 3072], P('dp'), may hold values from -0.25 to 0.25
Outputs:
- outcome: bfloat16 [8, 4, 4, 384, 3072], P('dp', 'ha', 'wa')
- query_grad: float32 [8, 4, 4, 384, 512], P('dp', 'ha', 'wa')
- key_grad: float32 [8, 4, 4, 384, 512], P('dp', 'ha', 'wa')
- value_grad: float32 [8, 4, 4, 384, 512], P('dp', 'ha', 'wa')
- weight_grad: float32 [512, 3072], P('dp')
All inputs are finite; a program needn't handle non-finite values.
Results may differ from a plain program's by a relative error of at most 0.035.
Values may be sent and summed in bfloat16 or wider, within the bound.
A program may use at most 192 MiB of HBM per device.

v0:
```python
import jax
import jax.numpy as jnp
from jax import lax
from jax.sharding import PartitionSpec as P

HEADS = 4


SCALE_POWER = -0.5


def shortened(array):
    return jax.tree.map(lambda a: a.astype(jnp.bfloat16) if a.dtype == jnp.float32 else a, array)


def shifted(value, axis, steps):
    count = lax.axis_size(axis)
    first, last = (max(0, -steps), min(count, count - steps))
    return lax.ppermute(value, axis, [(source, source + steps) for source in range(first, last)])


def with_halo(array, sides, width):
    for axis, dim in sides:
        peers, length = (lax.axis_size(axis), array.shape[dim])
        up = [(i, (i + 1) % peers) for i in range(peers - 1)]
        down = [(j, i) for i, j in up]
        last = lax.slice_in_dim(array, length - width, length, axis=dim)
        first = lax.slice_in_dim(array, 0, width, axis=dim)
        before = lax.ppermute(last, axis, up)
        after = lax.ppermute(first, axis, down)
        array = jnp.concatenate([before, array, after], axis=dim)
    return array


def product(pattern, first_op, second_op):
    return jnp.einsum(pattern, first_op, second_op, preferred_element_type=jnp.float32)


def stack_window(extended, tile_cols):
    window_parts = []
    for row_off in range(3):
        for col_off in range(3):
            window_parts.append(extended[row_off, col_off : col_off + tile_cols])
    stacked = jnp.stack(window_parts, axis=1)
    return stacked.reshape((tile_cols, 9 * stacked.shape[2]) + stacked.shape[3:])


def window_keep(row_ok, col_ok, tile_cols, tile_len):
    flag_list = []
    for row_off in range(3):
        for col_off in range(3):
            flag_list.append(
                jnp.logical_and(row_ok[row_off], col_ok[col_off : col_off + tile_cols])
            )
    stacked = jnp.stack(flag_list, axis=1)
    return jnp.repeat(stacked, tile_len, axis=1)


def spread_window(stacked, tile_cols, tile_len):
    window_parts = stacked.reshape((tile_cols, 3, 3, tile_len) + stacked.shape[2:])
    spread_rows = []
    for row_off in range(3):
        gathered = None
        for col_off in range(3):
            placed = jnp.pad(
                window_parts[:, row_off, col_off], ((col_off, 2 - col_off), (0, 0), (0, 0))
            )
            gathered = placed if gathered is None else gathered + placed
        spread_rows.append(gathered)
    return jnp.stack(spread_rows)


def widen_rim(edge_part, axis_pos, length, at_first):
    expanded = jnp.expand_dims(edge_part, axis_pos)
    pad_spec = [(0, 0)] * expanded.ndim
    pad_spec[axis_pos] = (0, length - 1) if at_first else (length - 1, 0)
    return jnp.pad(expanded, pad_spec)


def attend_row(query_row, key_ext, value_ext, visible, head_count):
    tile_cols, tile_len, feature_width = query_row.shape
    head_dim = feature_width // head_count
    score_scale = head_dim**SCALE_POWER
    query_heads = query_row.reshape(tile_cols, tile_len, head_count, head_dim)
    key_heads = stack_window(key_ext, tile_cols).reshape(
        tile_cols, 9 * tile_len, head_count, head_dim
    )
    value_heads = stack_window(value_ext, tile_cols).reshape(
        tile_cols, 9 * tile_len, head_count, head_dim
    )
    scores = product("jqhd,jkhd->jhqk", query_heads, key_heads) * score_scale
    scores = jnp.where(visible[:, None, None, :], scores, -1e30)
    row_max = jnp.max(scores, axis=-1, keepdims=True)
    log_norm = row_max + jnp.log(jnp.sum(jnp.exp(scores - row_max), axis=-1, keepdims=True))
    soft_probs = jnp.exp(scores - log_norm).astype(jnp.bfloat16)
    attended = product("jhqk,jkhd->jqhd", soft_probs, value_heads)
    attended = attended.reshape(tile_cols, tile_len, feature_width).astype(jnp.bfloat16)
    return (attended, soft_probs, log_norm[..., 0])


def query_back(query_row, key_ext, value_ext, attended, grad_attn, soft_probs, head_count):
    tile_cols, tile_len, feature_width = query_row.shape
    head_dim = feature_width // head_count
    score_scale = head_dim**SCALE_POWER
    attended_heads = attended.astype(jnp.float32).reshape(tile_cols, tile_len, head_count, head_dim)
    grad_heads = grad_attn.reshape(tile_cols, tile_len, head_count, head_dim)
    row_delta = jnp.sum(attended_heads * grad_heads.astype(jnp.float32), axis=-1)
    row_delta = jnp.transpose(row_delta, (0, 2, 1))
    value_heads = stack_window(value_ext, tile_cols).reshape(
        tile_cols, 9 * tile_len, head_count, head_dim
    )
    prob_grad = product("jqhd,jkhd->jhqk", grad_heads, value_heads)
    score_grad = (soft_probs.astype(jnp.float32) * (prob_grad - row_delta[..., None])).astype(
        jnp.bfloat16
    )
    key_heads = stack_window(key_ext, tile_cols).reshape(
        tile_cols, 9 * tile_len, head_count, head_dim
    )
    query_grad = product("jhqk,jkhd->jqhd", score_grad, key_heads) * score_scale
    query_grad = query_grad.reshape(tile_cols, tile_len, feature_width)
    query_heads = query_row.reshape(tile_cols, tile_len, head_count, head_dim)
    key_part = (product("jhqk,jqhd->jkhd", score_grad, query_heads) * score_scale).reshape(
        tile_cols, 9 * tile_len, feature_width
    )
    value_part = product("jhqk,jqhd->jkhd", soft_probs, grad_heads).reshape(
        tile_cols, 9 * tile_len, feature_width
    )
    return (
        query_grad,
        row_delta,
        spread_window(key_part, tile_cols, tile_len),
        spread_window(value_part, tile_cols, tile_len),
    )


def send_rows(edge_part, offset):
    return shifted(shortened(edge_part), "ha", offset).astype(edge_part.dtype)


def send_columns(edge_part, offset):
    return shifted(shortened(edge_part), "wa", offset).astype(edge_part.dtype)


def on_device(query_in, key_in, value_in, grad_out, out_weight):
    clip_count, tile_rows, tile_cols, tile_len, feature_width = query_in.shape
    model_width = grad_out.shape[-1]
    head_count = HEADS
    row_first = lax.axis_index("ha") * tile_rows
    col_first = lax.axis_index("wa") * tile_cols
    all_rows = tile_rows * lax.axis_size("ha")
    all_cols = tile_cols * lax.axis_size("wa")
    row_global = row_first - 1 + jnp.arange(tile_rows + 2, dtype=jnp.int32)
    row_flags = jnp.logical_and(row_global >= 0, row_global < all_rows)
    col_global = col_first - 1 + jnp.arange(tile_cols + 2, dtype=jnp.int32)
    col_ok = jnp.logical_and(col_global >= 0, col_global < all_cols)
    full_weight = lax.all_gather(out_weight, "dp", axis=0, tiled=True)
    flat_grad = grad_out.reshape(-1, model_width)
    grad_attn = lax.dot_general(
        flat_grad, full_weight, (((1,), (1,)), ((), ())), preferred_element_type=jnp.float32
    )
    grad_attn = grad_attn.astype(jnp.bfloat16).reshape(query_in.shape)
    extended = with_halo(jnp.stack([key_in, value_in]), (("ha", 2), ("wa", 3)), 1)
    key_ext_all = extended[0]
    value_ext_all = extended[1]
    row_total = clip_count * tile_rows
    flat_rows = jnp.arange(row_total, dtype=jnp.int32)
    query_rows = query_in.reshape(row_total, tile_cols, tile_len, feature_width)
    grad_rows = grad_attn.reshape(row_total, tile_cols, tile_len, feature_width)

    def row_window(extended_all):
        return extended_all[0]

    def row_keep():
        return window_keep(row_flags, col_ok, tile_cols, tile_len)

    def forward_row(inputs):
        query_row, flat_index = inputs
        return attend_row(
            query_row, row_window(key_ext_all), row_window(value_ext_all), row_keep(), head_count
        )

    attended, soft_probs, log_norm = lax.map(forward_row, (query_rows, flat_rows))
    flat_attn = attended.reshape(-1, feature_width)
    outcome = jnp.dot(flat_attn, full_weight, preferred_element_type=jnp.float32).astype(
        jnp.bfloat16
    )
    outcome = outcome.reshape(clip_count, tile_rows, tile_cols, tile_len, model_width)

    def query_side(inputs):
        query_row, grad_row, attended_row, probs_row, flat_index = inputs
        query_grad, row_delta, key_part, value_part = query_back(
            query_row,
            row_window(key_ext_all),
            row_window(value_ext_all),
            attended_row,
            grad_row,
            probs_row,
            head_count,
        )
        return (query_grad, jnp.stack([key_part, value_part]))

    query_grad, ext_parts = lax.map(
        query_side, (query_rows, grad_rows, attended, soft_probs, flat_rows)
    )
    ext_parts = ext_parts.reshape(
        clip_count, tile_rows, 2, 3, tile_cols + 2, tile_len, feature_width
    )
    padded_grad = None
    for row_off in range(3):
        placed = jnp.pad(
            ext_parts[:, :, :, row_off],
            ((0, 0), (row_off, 2 - row_off), (0, 0), (0, 0), (0, 0), (0, 0)),
        )
        padded_grad = placed if padded_grad is None else padded_grad + placed
    from_below = send_rows(padded_grad[:, 0], -1)
    from_above = send_rows(padded_grad[:, tile_rows + 1], 1)
    middle = padded_grad[:, 1 : tile_rows + 1]
    middle = (
        middle
        + widen_rim(from_below, 1, tile_rows, False)
        + widen_rim(from_above, 1, tile_rows, True)
    )
    from_right = send_columns(middle[:, :, :, 0], -1)
    from_left = send_columns(middle[:, :, :, tile_cols + 1], 1)
    core_part = middle[:, :, :, 1 : tile_cols + 1]
    core_part = (
        core_part
        + widen_rim(from_right, 3, tile_cols, False)
        + widen_rim(from_left, 3, tile_cols, True)
    )
    key_grad = core_part[:, :, 0]
    value_grad = core_part[:, :, 1]
    query_grad = query_grad.reshape(query_in.shape)
    row_share = feature_width // lax.axis_size("dp")
    local_term = lax.dot_general(
        flat_attn, flat_grad, (((0,), (0,)), ((), ())), preferred_element_type=jnp.float32
    )
    summed = lax.psum(local_term, ("dp", "ha", "wa"))
    weight_grad = lax.dynamic_slice_in_dim(summed, lax.axis_index("dp") * row_share, row_share, 0)
    return (outcome, query_grad, key_grad, value_grad, weight_grad)


def solution(mesh):
    return jax.shard_map(
        on_device,
        mesh=mesh,
        in_specs=(
            P("dp", "ha", "wa", None, None),
            P("dp", "ha", "wa", None, None),
            P("dp", "ha", "wa", None, None),
            P("dp", "ha", "wa", None, None),
            P("dp", None),
        ),
        out_specs=(
            P("dp", "ha", "wa", None, None),
            P("dp", "ha", "wa", None, None),
            P("dp", "ha", "wa", None, None),
            P("dp", "ha", "wa", None, None),
            P("dp", None),
        ),
        check_vma=False,
    )
```

profile of v0, /device:TPU:1, one launch (start us, length us, event | category | flops | bytes accessed | tf_op | source)
XLA Modules:
  0.0 475.2 jit_solution(9984312330930255074)
XLA Ops:
  15.0 15.3 %collective-permute-done.1 = bf16[2,1,1,1,384,512]{5,4,3,2,1,0:T(8,128)(2,1)S(1)} collective-permute-done((bf16[2,1,1,1,384,512]{5,4,3,2,1,0:T(8,128)(2,1)S(1)}, bf16[2,1,1,1,384,512]{5,4,3,2,1,0:T(8,128)(2,1)S(1)}, u32[]{:S(2)}, u32[]{:S(2)}) %collective-permute-start.1) | collective-permute-done | bytes 786464 | tf_op jit(solution)/shard_map/ppermute | solution.py:30
  53.8 16.4 %collective-permute-done.3 = bf16[2,1,3,1,384,512]{5,4,3,2,1,0:T(8,128)(2,1)} collective-permute-done((bf16[2,1,3,1,384,512]{5,4,3,2,1,0:T(8,128)(2,1)}, bf16[2,1,3,1,384,512]{5,4,3,2,1,0:T(8,128)(2,1)}, u32[]{:S(2)}, u32[]{:S(2)}) %collective-permute-start.3) | collective-permute-done | bytes 2359328 | tf_op jit(solution)/shard_map/ppermute | solution.py:30
  79.0 7.2 %reshape.242 = bf16[3456,4,128]{2,1,0:T(4,128)(2,1)} reshape(bf16[1,9,384,512]{3,2,1,0:T(8,128)(2,1)} %pad_maximum_fusion.2) | data formatting | bytes 7077888 | tf_op jit(solution)/shard_map/reshape.31
  86.3 6.9 %copy.102 = bf16[3456,4,128]{0,2,1:T(8,128)(2,1)} copy(bf16[3456,4,128]{2,1,0:T(4,128)(2,1)} %reshape.242) | data formatting | bytes 7077888 | tf_op jit(solution)/shard_map/reshape.31
  96.3 7.3 %reshape.241 = bf16[3456,4,128]{2,1,0:T(4,128)(2,1)} reshape(bf16[1,9,384,512]{3,2,1,0:T(8,128)(2,1)} %pad_maximum_fusion.1) | data formatting | bytes 7077888 | tf_op jit(solution)/shard_map/reshape.41
  103.6 7.5 %bitcast_reduce_fusion = (f32[4,384]{1,0:T(4,128)S(1)}, f32[4,3456,384]{2,1,0:T(8,128)S(1)}) fusion(pred[3456]{0:T(1024)(128)(4,1)S(1)} %broadcast_in_dim.69, bf16[3456,4,128]{0,2,1:T(8,128)(2,1)} %copy.102, bf16[384,4,128]{2,1,0:T(4,128)(2,1)S(1)} %copy-done.6), kind=kOutput, calls=%fused_computation.2 | convolution fusion | flops 1374878208 | bytes 25175424 | tf_op jit(solution)/shard_map/while/body/eval_jaxpr/jqhd,jkhd->jhqk/dot_general | solution.py:36
  116.8 7.9 %fusion.3 = bf16[4,384,3456]{1,2,0:T(8,128)(2,1)} fusion(f32[4,3456,384]{2,1,0:T(8,128)S(1)} %get-tuple-element.125, f32[4,384]{1,0:T(4,128)S(1)} %log_add_fusion, pred[3456]{0:T(1024)(128)(4,1)S(1)} %broadcast_in_dim.69), kind=kLoop, calls=%fused_computation.6 | loop fusion | flops 21233664 | bytes 31860096 | tf_op jit(solution)/shard_map/while/body/eval_jaxpr/convert_element_type | solution.py:95
  129.4 10.2 %convolution_bitcast_fusion = f32[1,3456,4,128]{1,3,2,0:T(8,128)} fusion(bf16[384,4,128]{0,2,1:T(8,128)(2,1)S(1)} %bitcast.185, bf16[4,384,3456]{1,2,0:T(8,128)(2,1)} %fusion.3), kind=kOutput, calls=%fused_computation.15 | convolution fusion | flops 1358954496 | bytes 18087936 | tf_op jit(solution)/shard_map/while/body/eval_jaxpr/jhqk,jqhd->jkhd/dot_general | solution.py:36
  139.6 6.3 %multiply_reduce_fusion = (f32[384,4]{0,1:T(4,128)S(1)}, bf16[4,128,384]{2,1,0:T(8,128)(2,1)S(1)}) fusion(f32[1,384,4,128]{1,3,2,0:T(8,128)S(1)} %bitcast.195, bf16[4,384,3456]{1,2,0:T(8,128)(2,1)} %fusion.3, bf16[3456,4,128]{2,1,0:T(4,128)(2,1)S(1)} %copy-done.2), kind=kOutput, calls=%fused_computation.75 | convolution fusion | flops 1359739392 | bytes 15341568 | tf_op jit(solution)/shard_map/while/body/eval_jaxpr/jhqk,jkhd->jqhd/dot_general | solution.py:36
  145.9 12.1 %multiply_convert_fusion = bf16[4,384,3456]{1,2,0:T(8,128)(2,1)} fusion(bf16[4,384,3456]{1,2,0:T(8,128)(2,1)} %fusion.3, bf16[384,4,128]{0,2,1:T(8,128)(2,1)S(1)} %bitcast.186, f32[4,384]{1,0:T(4,128)S(1)} %bitcast.197, bf16[3456,4,128]{2,1,0:T(4,128)(2,1)} %reshape.241), kind=kOutput, calls=%fused_computation.7 | convolution fusion | flops 1380188160 | bytes 25171968 | tf_op jit(solution)/shard_map/while/body/eval_jaxpr/jqhd,jkhd->jhqk/dot_general | solution.py:36
  158.0 9.1 %copy.108 = f32[1,3456,4,128]{3,2,0,1:T(4,128)} copy(f32[1,3456,4,128]{1,3,2,0:T(8,128)} %convolution_bitcast_fusion) | data formatting | bytes 14155776 | tf_op jit(solution)/shard_map/while/body/eval_jaxpr/jhqk,jqhd->jkhd/transpose | solution.py:36
  167.1 8.3 %slice_bitcast_fusion.23 = (f32[1,384,512]{2,0,1:T(1,128)S(1)}, f32[1,384,512]{2,0,1:T(1,128)}, f32[1,384,512]{2,0,1:T(1,128)}, f32[1,384,512]{2,0,1:T(1,128)}, ...) fusion(f32[1,3,3,384,512]{4,0,3,2,1:T(1,128)} %bitcast.183), kind=kLoop, calls=%fused_computation.64 | loop fusion | bytes 14155776 | tf_op jit(solution)/shard_map/while/body/eval_jaxpr/squeeze | solution.py:66
  178.4 15.1 %copy.105 = f32[1,3456,4,128]{3,2,0,1:T(4,128)S(1)} copy(f32[1,3456,4,128]{3,1,2,0:T(8,128)S(1)} %multiply_bitcast_fusion) | data formatting | bytes 14155776 | tf_op jit(solution)/shard_map/while/body/eval_jaxpr/mul | solution.py:122
  207.2 9.7 %maximum_bitcast_fusion.2 = f32[1,3,3,384,512]{4,2,3,1,0:T(4,128)} fusion(f32[1,3,384,512]{3,1,2,0:T(4,128)} %add_bitcast_fusion, f32[1,3,384,512]{3,1,2,0:T(4,128)} %add_bitcast_fusion.1, f32[1,3,384,512]{3,1,2,0:T(4,128)} %add_bitcast_fusion.2), kind=kLoop, calls=%fused_computation.12 | loop fusion | flops 3538944 | bytes 14155776 | tf_op jit(solution)/shard_map/while/body/eval_jaxpr/stack | solution.py:200
  228.1 9.7 %maximum_bitcast_fusion.1 = f32[1,3,3,384,512]{4,2,3,1,0:T(4,128)} fusion(f32[1,3,384,512]{3,1,2,0:T(4,128)} %add_bitcast_fusion.3, f32[1,3,384,512]{3,1,2,0:T(4,128)} %add_bitcast_fusion.4, f32[1,3,384,512]{3,1,2,0:T(4,128)} %add_bitcast_fusion.5), kind=kLoop, calls=%fused_computation.11 | loop fusion | flops 3538944 | bytes 14155776 | tf_op jit(solution)/shard_map/while/body/eval_jaxpr/stack | solution.py:200
  237.7 10.5 %maximum_bitcast_fusion = f32[1,1,2,3,3,384,512]{6,4,5,3,2,1,0:T(4,128)S(1)} fusion(f32[1,3,3,384,512]{4,2,3,1,0:T(4,128)} %maximum_bitcast_fusion.2, f32[1,3,3,384,512]{4,2,3,1,0:T(4,128)} %maximum_bitcast_fusion.1), kind=kLoop, calls=%fused_computation.9 | loop fusion | flops 3538944 | bytes 28311552 | tf_op jit(solution)/shard_map/reshape | solution.py:205
  248.2 7.7 %slice_bitcast_fusion.2 = (f32[1,1,2,3,384,512]{5,3,4,2,1,0:T(4,128)}, f32[1,1,2,3,384,512]{5,3,4,2,1,0:T(4,128)}, f32[1,1,2,3,384,512]{5,3,4,2,1,0:T(4,128)}) fusion(f32[1,1,2,3,3,384,512]{6,4,5,3,2,1,0:T(4,128)S(1)} %maximum_bitcast_fusion), kind=kLoop, calls=%fused_computation.20 | loop fusion | bytes 28311552 | tf_op jit(solution)/shard_map/squeeze | solution.py:211
  255.9 18.2 %pad_add_fusion = (f32[1,3,2,3,384,512]{5,3,4,2,1,0:T(4,128)}, bf16[1,3,2,3,384,512]{5,3,4,2,1,0:T(4,128)(2,1)S(1)}) fusion(f32[1,1,2,3,384,512]{5,3,4,2,1,0:T(4,128)} %get-tuple-element.86, f32[1,1,2,3,384,512]{5,3,4,2,1,0:T(4,128)} %get-tuple-element.87, f32[1,1,2,3,384,512]{5,3,4,2,1,0:T(4,128)} %get-tuple-element.85), kind=kLoop, calls=%fused_computation.10 | loop fusion | flops 10616832 | bytes 35389440 | tf_op jit(solution)/shard_map/add | solution.py:214
  291.5 33.2 %collective-permute-done.5 = bf16[1,2,3,384,512]{4,3,2,1,0:T(8,128)(2,1)} collective-permute-done((bf16[1,2,3,384,512]{4,3,2,1,0:T(8,128)(2,1)}, bf16[1,2,3,384,512]{4,3,2,1,0:T(8,128)(2,1)}, u32[]{:S(2)}, u32[]{:S(2)}) %collective-permute-start.5) | collective-permute-done | bytes 2359328 | tf_op jit(solution)/shard_map/ppermute | solution.py:19
  324.7 10.2 %collective-permute-done.4 = bf16[1,2,3,384,512]{4,3,2,1,0:T(8,128)(2,1)} collective-permute-done((bf16[1,2,3,384,512]{4,3,2,1,0:T(8,128)(2,1)}, bf16[1,2,3,384,512]{4,3,2,1,0:T(8,128)(2,1)}, u32[]{:S(2)}, u32[]{:S(2)}) %collective-permute-start.4) | collective-permute-done | bytes 2359328 | tf_op jit(solution)/shard_map/ppermute | solution.py:19
  335.0 10.9 %fusion.24 = (bf16[1,1,2,3,384,512]{5,3,4,2,1,0:T(4,128)(2,1)S(1)}, f32[1,1,2,3,384,512]{5,3,4,2,1,0:T(4,128)}) fusion(bf16[1,2,3,384,512]{4,3,2,1,0:T(8,128)(2,1)} %collective-permute-done.5, bf16[1,2,3,384,512]{4,3,2,1,0:T(8,128)(2,1)} %collective-permute-done.4, f32[1,3,2,3,384,512]{5,3,4,2,1,0:T(4,128)} %get-tuple-element.83), kind=kLoop, calls=%fused_computation.84 | loop fusion | flops 5898240 | bytes 16515072 | tf_op jit(solution)/shard_map/convert.6
  354.8 7.1 %convolution_multiply_fusion = f32[4,128,384]{2,1,0:T(8,128)} fusion(bf16[3456,4,128]{0,2,1:T(8,128)(2,1)S(1)} %copy-done.3, bf16[4,384,3456]{1,2,0:T(8,128)(2,1)} %multiply_convert_fusion), kind=kOutput, calls=%fused_computation.45 | convolution fusion | flops 1359151104 | bytes 14942208 | tf_op jit(solution)/shard_map/while/body/eval_jaxpr/jhqk,jkhd->jqhd/dot_general | solution.py:36
  368.9 87.0 %all-reduce.23.cloned.1.call-done = f32[512,3072]{1,0:T(8,128)} async-done(((f32[512,3072]{1,0:T(8,128)}), f32[512,3072]{1,0:T(8,128)}) %all-reduce.23.cloned.1.call-update) | async-done | bytes 6291472 | tf_op jit(solution)/shard_map/psum | solution.py:238
  458.0 7.0 %fusion.13 = f32[1,1,2,1,384,512]{5,3,4,2,1,0:T(1,128)S(1)} fusion(f32[1,1,2,3,384,512]{5,3,4,2,1,0:T(4,128)} %get-tuple-element.82, bf16[1,1,2,384,512]{4,0,3,2,1:T(2,128)(2,1)} %collective-permute-done.7, bf16[1,1,2,384,512]{4,0,3,2,1:T(2,128)(2,1)} %collective-permute-done.6), kind=kLoop, calls=%fused_computation.44 | loop fusion | flops 1572864 | bytes 4718592 | tf_op jit(solution)/shard_map/add | solution.py:227
  (98 shorter events, 108.4 us)
Async XLA Ops:
  7.2 117.6 %copy-start = (bf16[1,1,1,384,3072]{4,3,2,1,0:T(8,128)(2,1)S(1)}, bf16[1,1,1,384,3072]{4,3,2,1,0:T(8,128)(2,1)}, u32[]{:S(2)}) copy-start(bf16[1,1,1,384,3072]{4,3,2,1,0:T(8,128)(2,1)} %param.8) | copy-start | bytes 7077892
  7.2 45.8 %copy-start.21 = (bf16[1,1,1,384,512]{4,3,2,1,0:T(8,128)(2,1)S(1)}, bf16[1,1,1,384,512]{4,3,2,1,0:T(8,128)(2,1)}, u32[]{:S(2)}) copy-start(bf16[1,1,1,384,512]{4,3,2,1,0:T(8,128)(2,1)} %param.5) | copy-start | bytes 1179652
  7.2 117.5 %all-gather.2.cloned.1.call-start = ((), (), s32[]{:S(2)}) async-start(), calls=%async_computation | async-start | bytes 3538944 | tf_op jit(solution)/shard_map/all_gather | solution.py:156
  7.2 63.8 %copy-start.4 = (bf16[1,1,1,384,512]{4,3,2,1,0:T(8,128)(2,1)S(1)}, bf16[1,1,1,384,512]{4,3,2,1,0:T(8,128)(2,1)}, u32[]{:S(2)}) copy-start(bf16[1,1,1,384,512]{4,3,2,1,0:T(8,128)(2,1)} %param.7) | copy-start | bytes 1179652
  7.2 63.8 %copy-start.5 = (bf16[1,1,1,384,512]{4,3,2,1,0:T(8,128)(2,1)S(1)}, bf16[1,1,1,384,512]{4,3,2,1,0:T(8,128)(2,1)}, u32[]{:S(2)}) copy-start(bf16[1,1,1,384,512]{4,3,2,1,0:T(8,128)(2,1)} %param.6) | copy-start | bytes 1179652
  8.6 21.6 %collective-permute-start.1 = (bf16[2,1,1,1,384,512]{5,4,3,2,1,0:T(8,128)(2,1)S(1)}, bf16[2,1,1,1,384,512]{5,4,3,2,1,0:T(8,128)(2,1)S(1)}, u32[]{:S(2)}, u32[]{:S(2)}) collective-permute-start(bf16[2,1,1,1,384,512]{5,4,3,2,1,0:T(8,128)(2,1)S(1)} %pad_maximum_fusion.4), channel_id=1, source_target_pairs={{4,0},{8,4},{12,8},{5,1},{9,5},{13,9},{6,2},{10,6},{14,10},{7,3},{... | collective-permute-start | bytes 2359304 | tf_op jit(solution)/shard_map/ppermute | solution.py:30
  9.9 21.2 %collective-permute-start = (bf16[2,1,1,1,384,512]{5,4,3,2,1,0:T(8,128)(2,1)S(1)}, bf16[2,1,1,1,384,512]{5,4,3,2,1,0:T(8,128)(2,1)S(1)}, u32[]{:S(2)}, u32[]{:S(2)}) collective-permute-start(bf16[2,1,1,1,384,512]{5,4,3,2,1,0:T(8,128)(2,1)S(1)} %pad_maximum_fusion.4), channel_id=1, source_target_pairs={{0,4},{4,8},{8,12},{1,5},{5,9},{9,13},{2,6},{6,10},{10,14},{3,7},{... | collective-permute-start | bytes 2359304 | tf_op jit(solution)/shard_map/ppermute | solution.py:29
  34.2 36.0 %collective-permute-start.3 = (bf16[2,1,3,1,384,512]{5,4,3,2,1,0:T(8,128)(2,1)}, bf16[2,1,3,1,384,512]{5,4,3,2,1,0:T(8,128)(2,1)}, u32[]{:S(2)}, u32[]{:S(2)}) collective-permute-start(bf16[2,1,3,1,384,512]{5,4,3,2,1,0:T(8,128)(2,1)} %pad_maximum_fusion.3), channel_id=1, source_target_pairs={{1,0},{2,1},{3,2},{5,4},{6,5},{7,6},{9,8},{10,9},{11,10},{13,12},{... | collective-permute-start | bytes 7077896 | tf_op jit(solution)/shard_map/ppermute | solution.py:30
  37.6 33.4 %collective-permute-start.2 = (bf16[2,1,3,1,384,512]{5,4,3,2,1,0:T(8,128)(2,1)}, bf16[2,1,3,1,384,512]{5,4,3,2,1,0:T(8,128)(2,1)}, u32[]{:S(2)}, u32[]{:S(2)}) collective-permute-start(bf16[2,1,3,1,384,512]{5,4,3,2,1,0:T(8,128)(2,1)} %pad_maximum_fusion.3), channel_id=1, source_target_pairs={{0,1},{1,2},{2,3},{4,5},{5,6},{6,7},{8,9},{9,10},{10,11},{12,13},{... | collective-permute-start | bytes 7077896 | tf_op jit(solution)/shard_map/ppermute | solution.py:29
  40.8 415.1 %all-reduce.23.cloned.1.call-start = ((), (), s32[]{:S(2)}) async-start(), calls=%async_computation.1 | async-start | bytes 12582912 | tf_op jit(solution)/shard_map/psum | solution.py:238
  96.3 7.3 %copy-start.6 = (bf16[384,4,128]{2,1,0:T(4,128)(2,1)S(1)}, bf16[384,4,128]{2,1,0:T(4,128)(2,1)}, u32[]{:S(2)}) copy-start(bf16[384,4,128]{2,1,0:T(4,128)(2,1)} %reshape.243) | copy-start | bytes 1179652
  129.3 10.3 %copy-start.2 = (bf16[3456,4,128]{2,1,0:T(4,128)(2,1)S(1)}, bf16[3456,4,128]{2,1,0:T(4,128)(2,1)}, u32[]{:S(2)}) copy-start(bf16[3456,4,128]{2,1,0:T(4,128)(2,1)} %reshape.241) | copy-start | bytes 10616836
  129.3 10.3 %copy-start.7 = (f32[384,512]{0,1:T(8,128)S(1)}, f32[384,512]{0,1:T(8,128)}, u32[]{:S(2)}) copy-start(f32[384,512]{0,1:T(8,128)} %copy.100) | copy-start | bytes 2359300
  167.1 8.3 %copy-start.1 = (bf16[4,384,3456]{1,2,0:T(8,128)(2,1)S(1)}, bf16[4,384,3456]{1,2,0:T(8,128)(2,1)}, u32[]{:S(2)}) copy-start(bf16[4,384,3456]{1,2,0:T(8,128)(2,1)} %multiply_convert_fusion) | copy-start | bytes 31850500
  193.5 4.2 copy-start.18
  193.5 4.2 copy-start.19
  216.9 4.6 copy-start.13
  216.9 4.6 copy-start.14
  216.9 4.6 copy-start.15
  278.3 46.4 %collective-permute-start.5 = (bf16[1,2,3,384,512]{4,3,2,1,0:T(8,128)(2,1)}, bf16[1,2,3,384,512]{4,3,2,1,0:T(8,128)(2,1)}, u32[]{:S(2)}, u32[]{:S(2)}) collective-permute-start(bf16[1,2,3,384,512]{4,3,2,1,0:T(8,128)(2,1)} %copy.113), channel_id=1, source_target_pairs={{0,4},{4,8},{8,12},{1,5},{5,9},{9,13},{2,6},{6,10},{10,14},{3,7},{... | collective-permute-start | bytes 7077896 | tf_op jit(solution)/shard_map/ppermute | solution.py:19
  285.7 49.3 %collective-permute-start.4 = (bf16[1,2,3,384,512]{4,3,2,1,0:T(8,128)(2,1)}, bf16[1,2,3,384,512]{4,3,2,1,0:T(8,128)(2,1)}, u32[]{:S(2)}, u32[]{:S(2)}) collective-permute-start(bf16[1,2,3,384,512]{4,3,2,1,0:T(8,128)(2,1)} %copy.111), channel_id=1, source_target_pairs={{4,0},{8,4},{12,8},{5,1},{9,5},{13,9},{6,2},{10,6},{14,10},{7,3},{... | collective-permute-start | bytes 7077896 | tf_op jit(solution)/shard_map/ppermute | solution.py:19
  345.9 8.9 %copy-start.3 = (bf16[3456,4,128]{0,2,1:T(8,128)(2,1)S(1)}, bf16[3456,4,128]{0,2,1:T(8,128)(2,1)}, u32[]{:S(2)}) copy-start(bf16[3456,4,128]{0,2,1:T(8,128)(2,1)} %copy.102) | copy-start | bytes 10616836
  349.3 108.7 %collective-permute-start.7 = (bf16[1,1,2,384,512]{4,0,3,2,1:T(2,128)(2,1)}, bf16[1,1,2,384,512]{4,0,3,2,1:T(2,128)(2,1)}, u32[]{:S(2)}, u32[]{:S(2)}) collective-permute-start(bf16[1,1,2,384,512]{4,0,3,2,1:T(2,128)(2,1)} %get-tuple-element.115), channel_id=1, source_target_pairs={{0,1},{1,2},{2,3},{4,5},{5,6},{6,7},{8,9},{9,10},{10,11},{12,13},{... | collective-permute-start | bytes 2359304 | tf_op jit(solution)/shard_map/ppermute | solution.py:19
  351.3 106.7 %collective-permute-start.6 = (bf16[1,1,2,384,512]{4,0,3,2,1:T(2,128)(2,1)}, bf16[1,1,2,384,512]{4,0,3,2,1:T(2,128)(2,1)}, u32[]{:S(2)}, u32[]{:S(2)}) collective-permute-start(bf16[1,1,2,384,512]{4,0,3,2,1:T(2,128)(2,1)} %get-tuple-element.114), channel_id=1, source_target_pairs={{1,0},{2,1},{3,2},{5,4},{6,5},{7,6},{9,8},{10,9},{11,10},{13,12},{... | collective-permute-start | bytes 2359304 | tf_op jit(solution)/shard_map/ppermute | solution.py:19
  (8 other events, 25.0 us)
Sparse Core Ops, SparseCore 0:
  40.9 66.9 all-gather.1
  291.6 164.2 all-reduce.22
where the time goes:
time: 483 us; the launch traced here: 475 us
  waiting for transfers between devices  164 us (34%)
  other arithmetic  114 us (24%)
  local copies, waits for them, and re-layouts  87.8 us (18%)
  matrix products  58.6 us (12%)
  between operations  26.1 us (5%)
  starting transfers between devices  25.1 us (5%)
    psum x1, waiting for transfers between devices, on_device(): summed = lax.psum(local_term, ('dp', 'ha', 'wa'))  87 us
    dot_general x6, matrix products, product(): jnp.einsum(pattern, first_op, second_op, preferred_element_type=jnp.float32)  46.1 us
    ppermute x4, waiting for transfers between devices, shifted(): lax.ppermute(value, axis, [(source, source + steps) for source in range(f...  43.5 us
    ppermute x2, waiting for transfers between devices, with_halo(): after = lax.ppermute(first, axis, down)  31.6 us
    another operation x5, local copies, waits for them, and re-layouts  22.4 us
    another operation x6, other arithmetic, spread_window(): return jnp.stack(spread_rows)  20.7 us
    another operation x2, other arithmetic, query_side(): return (query_grad, jnp.stack([key_part, value_part]))  19.4 us
    add x1, other arithmetic, on_device(): padded_grad = placed if padded_grad is None else padded_grad + placed  18.2 us
  transfers between devices with their start and end apart: 10, of which 7 were waited for; matrix products, arithmetic and copies ran while one was open for 19% of the time, Pallas kernels for 0%

commit v1 on v0

v1 whole, which is shorter than its diff:
```python
import math

import jax
import jax.numpy as jnp
from jax import lax
from jax.experimental import pallas as pl
from jax.experimental.pallas import tpu as pltpu
from jax.sharding import PartitionSpec as P

MESH = pl.DeviceIdType.MESH
BF = jnp.bfloat16
F32 = jnp.float32

TILE, HD, FEAT, D = 384, 128, 512, 3072
HALF, QUART = D // 2, D // 4
SCALE = HD**-0.5
EXP_SCALE = SCALE * math.log2(math.e)


def dot_nn(a, b):
    return lax.dot_general(a, b, (((1,), (0,)), ((), ())), preferred_element_type=F32)


def dot_nt(a, b):
    return lax.dot_general(a, b, (((1,), (1,)), ((), ())), preferred_element_type=F32)


def dot_tn(a, b):
    return lax.dot_general(a, b, (((0,), (0,)), ((), ())), preferred_element_type=F32)


def flip(v):
    return v + 1 - 2 * lax.rem(v, 2)


def unit_index(t, b):
    return 3 * t + b - 1 - lax.rem(t, 2) * (1 - lax.div(t, 2))


N_SEND, N_RECV = 96, 96


def kernel(
    q_in, k_in, v_in, g_in, w_in,
    out_o, dq_o, dk_o, dv_o, wg_o,
    qg, kg, vg, s_ref, sc_ref, m_ref, p_ref, pc_ref, o_acc, linv, ob, dog, dop, delta,
    dq, dk, dv, ys, zs, cs, yr, zr, cr, dqb, dkb, dvb, att, gat, gat_acc, gov, ws, oc,
    acc, tsend, trecv, xs, xa, xb, xr, rsum, y3s, y3r, y4s, y4r, z4s, z4r, fin,
    ssem, rsem, lsem,
):
    dp, z, wa = lax.axis_index("dp"), lax.axis_index("ha"), lax.axis_index("wa")
    x, yh = lax.rem(dp, 4), lax.div(dp, 4)
    c, ylo = lax.rem(wa, 2), lax.div(wa, 2)
    i, j = lax.rem(lax.div(z + 1, 2), 2), lax.rem(lax.div(wa + 1, 2), 2)
    t_me = 2 * i + j
    zp, wp = flip(z), flip(wa)
    peers = {1: (dp, z, wp), 2: (dp, zp, wa), 3: (dp, zp, wp)}
    peer_t = {0: t_me, 1: 2 * i + 1 - j, 2: 2 * (1 - i) + j, 3: 2 * (1 - i) + 1 - j}
    dev_y, dev_z, dev_c = (dp, z, 3 - wa), (dp, 3 - z, wa), (dp, 3 - z, 3 - wa)
    xp_i, xm_i, x2_i = lax.rem(x + 1, 4), lax.rem(x + 3, 4), lax.rem(x + 2, 4)
    dev_xp, dev_xm = (yh * 4 + xp_i, z, wa), (yh * 4 + xm_i, z, wa)
    dev_yi = (lax.rem(dp + 4, 8), z, lax.rem(wa + 2, 4))
    dev_core = peers[1]
    dev_ylo = (dp, z, lax.rem(wa + 2, 4))
    clip_devs = [
        (dp, lax.rem(z + a, 4), lax.rem(wa + b, 4)) for a in range(4) for b in range(4) if a or b
    ]
    fl = 4 * (1 - yh)

    sends = []
    counts = {"s": 0, "r": 0, "l": 0}

    def new(kind, n=1):
        first = counts[kind]
        counts[kind] += n
        return first

    def send(src, dst, dev, r):
        copy = pltpu.make_async_remote_copy(
            src, dst, ssem.at[new("s")], rsem.at[r], device_id=dev, device_id_type=MESH
        )
        copy.start()
        sends.append(copy)

    def local(src, dst, sem):
        pltpu.make_async_copy(src, dst, sem).start()

    def arrived(dst, r):
        pltpu.make_async_copy(dst, dst, rsem.at[r]).wait()

    def cols(n, width=HD):
        return pl.ds(pl.multiple_of(n * width, width), width)

    barrier = pltpu.get_barrier_semaphore()
    neighbours = clip_devs + [dev_xp, dev_xm, dev_yi]
    for dev in neighbours:
        pl.semaphore_signal(barrier, inc=1, device_id=dev, device_id_type=MESH)

    l_g, l_w = new("l"), new("l")
    local(g_in, gov, lsem.at[l_g])
    local(w_in, ws.at[dp], lsem.at[l_w])
    r_k, r_q, r_v = new("r", 4), new("r", 4), new("r", 4)
    local(k_in.at[:, cols(t_me)], kg.at[2 + t_me], rsem.at[r_k + t_me])
    local(q_in.at[:, cols(t_me)], qg.at[t_me], rsem.at[r_q + t_me])
    local(v_in.at[:, cols(t_me)], vg.at[2 + t_me, :, pl.ds(0, HD)], rsem.at[r_v + t_me])
    pl.semaphore_wait(barrier, len(neighbours))

    for n in (2, 3, 1):
        send(k_in.at[:, cols(peer_t[n])], kg.at[2 + t_me], peers[n], r_k + t_me)
    hc = pl.ds(pl.multiple_of(c * HALF, HALF), HALF)
    hca = pl.ds(pl.multiple_of(c * HALF, HALF), QUART)
    hcb = pl.ds(pl.multiple_of(c * HALF + QUART, QUART), QUART)
    hall = pl.ds(0, 64)
    r_w = new("r", 8)
    r_wc = new("r", 7)
    send(w_in.at[hall, hc], ws.at[dp, hall, hc], dev_xp, r_w + 0)
    send(w_in.at[hall, hc], ws.at[dp, hall, hc], dev_xm, r_w + 1)
    send(w_in.at[hall, hc], ws.at[dp, hall, hc], dev_yi, r_w + 2)
    for n in (2, 3, 1):
        send(q_in.at[:, cols(peer_t[n])], qg.at[t_me], peers[n], r_q + t_me)
    for n in (2, 3, 1):
        send(v_in.at[:, cols(peer_t[n])], vg.at[2 + t_me, :, pl.ds(0, HD)], peers[n], r_v + t_me)

    def ones(s, _):
        vg[s, :, HD:] = jnp.ones((TILE, HD), BF)
        return 0

    lax.fori_loop(0, 9, ones, 0)
    m_ref[...] = jnp.full(m_ref.shape, -jnp.inf, F32)
    dq[...] = jnp.zeros(dq.shape, F32)
    dk[...] = jnp.zeros(dk.shape, F32)
    dv[...] = jnp.zeros(dv.shape, F32)

    def halo_of(buf, r_own, width, r_halo):
        def at(s):
            return buf.at[s] if width is None else buf.at[s, :, pl.ds(0, width)]

        for s in (3, 5, 4, 2):
            arrived(at(s), r_own + s - 2)
            if s == 3:
                send(at(3), at(6), dev_y, r_halo + 2)
            if s == 5:
                send(at(5), at(7), dev_y, r_halo + 3)
                send(at(5), at(1), dev_z, r_halo + 1)
                send(at(5), at(8), dev_c, r_halo + 4)
            if s == 4:
                send(at(4), at(0), dev_z, r_halo + 0)

    def w_at(d, columns):
        return ws.at[d, hall, columns]

    d_xm, d_xp, d_x2 = yh * 4 + xm_i, yh * 4 + xp_i, yh * 4 + x2_i
    f_x, f_xm, f_xp, f_x2 = fl + x, fl + xm_i, fl + xp_i, fl + x2_i

    r_kh, r_vh = new("r", 5), new("r", 5)
    halo_of(kg, r_k, None, r_kh)

    arrived(w_at(d_xm, hc), r_w + 0)
    send(w_at(d_xm, hca), w_at(d_xm, hca), dev_xp, r_w + 3)
    send(w_at(d_xm, hc), w_at(d_xm, hc), dev_core, r_wc + 0)
    arrived(w_at(d_xp, hc), r_w + 1)
    send(w_at(d_xp, hcb), w_at(d_xp, hcb), dev_xm, r_w + 4)
    send(w_at(d_xp, hc), w_at(d_xp, hc), dev_core, r_wc + 1)
    arrived(w_at(f_x, hc), r_w + 2)
    send(w_at(f_x, hc), w_at(f_x, hc), dev_xp, r_w + 5)
    send(w_at(f_x, hc), w_at(f_x, hc), dev_xm, r_w + 6)
    send(w_at(f_x, hc), w_at(f_x, hc), dev_core, r_wc + 2)

    for s in range(4):
        arrived(qg.at[s], r_q + s)

    def scores(t, b):
        s = dot_nt(qg[t], kg[pl.ds(2 * b, 2)].reshape(2 * TILE, HD))
        s_ref[unit_index(t, b)] = s
        m = m_ref[t]
        for n in range(6):
            m = jnp.maximum(m, s[:, n * HD : (n + 1) * HD])
        m_ref[t] = m

    def own_scores(n, _):
        scores(lax.div(n, 2), 1 + lax.rem(n, 2))
        return 0

    lax.fori_loop(0, 8, own_scores, 0)

    arrived(w_at(d_x2, hca), r_w + 3)
    arrived(w_at(d_x2, hcb), r_w + 4)
    send(w_at(d_x2, hc), w_at(d_x2, hc), dev_yi, r_w + 7)
    send(w_at(d_x2, hc), w_at(d_x2, hc), dev_core, r_wc + 3)

    for s, r in ((0, 0), (1, 1), (6, 2), (7, 3), (8, 4)):
        arrived(kg.at[s], r_kh + r)

    def halo_scores(n, _):
        late = lax.div(n, 2)
        scores(jnp.where(late == 0, 1 + 2 * n, n), 3 - 3 * late)
        return 0

    lax.fori_loop(0, 4, halo_scores, 0)
    s = dot_nt(qg[3], kg[8])
    sc_ref[...] = s
    m_ref[3] = jnp.maximum(
        jnp.maximum(m_ref[3], s[:, :HD]), jnp.maximum(s[:, HD : 2 * HD], s[:, 2 * HD :])
    )

    halo_of(vg, r_v, HD, r_vh)

    def weigh(t, low, high):
        m = jnp.max(m_ref[t], axis=-1, keepdims=True) * EXP_SCALE

        def block(b, _):
            u = unit_index(t, b)
            p = jnp.exp2(s_ref[u] * EXP_SCALE - m).astype(BF)
            p_ref[u] = p
            o_acc[...] += dot_nn(p, vg[pl.ds(2 * b, 2)].reshape(2 * TILE, 2 * HD))
            return 0

        o_acc[...] = jnp.zeros(o_acc.shape, F32)
        lax.fori_loop(low, high, block, 0)
        return m

    def attend(t):
        inverse = 1.0 / o_acc[:, HD:]
        linv[t] = inverse
        ob[t] = (o_acc[:, :HD] * inverse).astype(BF)

    t0 = jnp.int32(0)
    weigh(t0, 1, 3)
    attend(t0)

    arrived(w_at(f_xm, hc), r_w + 5)
    send(w_at(f_xm, hc), w_at(f_xm, hc), dev_core, r_wc + 4)
    arrived(w_at(f_xp, hc), r_w + 6)
    send(w_at(f_xp, hc), w_at(f_xp, hc), dev_core, r_wc + 5)
    arrived(w_at(f_x2, hc), r_w + 7)
    send(w_at(f_x2, hc), w_at(f_x2, hc), dev_core, r_wc + 6)

    for s, r in ((0, 0), (1, 1), (6, 2), (7, 3), (8, 4)):
        arrived(vg.at[s, :, pl.ds(0, HD)], r_vh + r)
    weigh(t0 + 1, 1, 4)
    attend(t0 + 1)
    weigh(t0 + 2, 0, 3)
    attend(t0 + 2)
    m = weigh(t0 + 3, 0, 4)
    p = jnp.exp2(sc_ref[...] * EXP_SCALE - m).astype(BF)
    pc_ref[...] = p
    o_acc[...] += dot_nn(p, vg[8])
    attend(t0 + 3)

    r_o = new("r", 4)
    local(ob.at[t_me], att.at[:, cols(t_me)], rsem.at[r_o + t_me])
    for n in (2, 3, 1):
        send(ob.at[peer_t[n]], att.at[:, cols(t_me)], peers[n], r_o + t_me)

    pltpu.make_async_copy(g_in, gov, lsem.at[l_g]).wait()
    pltpu.make_async_copy(w_in, ws.at[dp], lsem.at[l_w]).wait()
    hc_o = pl.ds(pl.multiple_of((1 - c) * HALF, HALF), HALF)
    for n, d in enumerate((d_xm, d_xp, f_x, d_x2, f_xm, f_xp, f_x2)):
        arrived(w_at(d, hc_o), r_wc + n)
    gat_acc[...] = jnp.zeros(gat_acc.shape, F32)

    def grad_block(n, _):
        wide = pl.ds(pl.multiple_of(n * 512, 512), 512)
        gat_acc[...] += dot_nt(gov[:, wide], ws[:, :, wide].reshape(FEAT, 512))
        return 0

    lax.fori_loop(0, 6, grad_block, 0)
    gat[...] = gat_acc[...].astype(BF)
    r_g = new("r", 4)
    local(gat.at[:, cols(t_me)], dog.at[t_me], rsem.at[r_g + t_me])
    for n in (2, 3, 1):
        send(gat.at[:, cols(peer_t[n])], dog.at[t_me], peers[n], r_g + t_me)

    for s in range(4):
        arrived(att.at[:, cols(s)], r_o + s)

    def term_block(n, into, half):
        wide = pl.ds(pl.multiple_of(half * HALF + n * 512, 512), 512)
        to = pl.ds(pl.multiple_of(n * 512, 512), 512)
        d = dot_tn(att[...], gov[:, wide])
        for h in range(2):
            for xx in range(4):
                first = h * 256 + xx * 64
                into[xx, h, :, to] = d[first : first + 64].astype(into.dtype)

    def other_half(n, _):
        term_block(n, tsend, 1 - c)
        return 0

    def own_half(n, _):
        term_block(n, acc, c)
        return 0

    lax.fori_loop(0, 3, other_half, 0)
    r_t = new("r")
    send(tsend, trecv, dev_core, r_t)
    lax.fori_loop(0, 3, own_half, 0)

    arrived(trecv, r_t)

    def add_core(n, _):
        s = acc[n] + trecv[n].astype(F32)
        acc[n] = s
        xs[n] = s.astype(BF)
        return 0

    lax.fori_loop(0, 4, add_core, 0)
    two, rows = pl.ds(0, 2), pl.ds(0, 64)
    ca, cb = pl.ds(0, QUART), pl.ds(QUART, QUART)
    r_xa, r_xr = new("r", 2), new("r", 4)
    send(xs.at[x2_i, two, rows, ca], xa.at[0], dev_xp, r_xa)
    send(xs.at[x2_i, two, rows, cb], xa.at[1], dev_xm, r_xa + 1)
    send(xs.at[xp_i, two, rows, cb], xr.at[2], dev_xp, r_xr + 2)
    send(xs.at[xm_i, two, rows, ca], xr.at[3], dev_xm, r_xr + 3)

    for s in range(4):
        arrived(dog.at[s], r_g + s)

    def prepare(t, _):
        scaled = (dog[t].astype(F32) * linv[t]).astype(BF)
        dop[t] = scaled
        d = jnp.sum(ob[t].astype(F32) * scaled.astype(F32), axis=-1, keepdims=True)
        delta[t] = jnp.broadcast_to(d, (TILE, HD))
        return 0

    lax.fori_loop(0, 4, prepare, 0)

    def back(t, b):
        p = p_ref[unit_index(t, b)]
        keys = kg[pl.ds(2 * b, 2)].reshape(2 * TILE, HD)
        values = vg[pl.ds(2 * b, 2), :, :HD].reshape(2 * TILE, HD)
        dprob = dot_nt(dop[t], values)
        ds = (p.astype(F32) * (dprob - delta[t][:, :1])).astype(BF)
        dq[t] += dot_nn(ds, keys)
        dk[b] += dot_tn(ds, qg[t])
        dv[b] += dot_tn(p, dop[t])

    p = pc_ref[...]
    dprob = dot_nt(dop[3], vg[8, :, :HD])
    ds = (p.astype(F32) * (dprob - delta[3][:, :1])).astype(BF)
    dq[3] += dot_nn(ds, kg[8])
    cs[0] = (dot_tn(ds, qg[3]) * SCALE).astype(BF)
    cs[1] = dot_tn(p, dop[3]).astype(BF)
    r_cb, r_yb, r_zb = new("r"), new("r"), new("r")
    send(cs, cr, dev_c, r_cb)

    def back_y(n, _):
        back(1 + 2 * n, jnp.int32(3))
        return 0

    lax.fori_loop(0, 2, back_y, 0)
    ys[0] = (dk[3] * SCALE).astype(BF)
    ys[1] = dv[3].astype(BF)
    send(ys, yr, dev_y, r_yb)

    def back_z(n, _):
        back(2 + n, jnp.int32(0))
        return 0

    lax.fori_loop(0, 2, back_z, 0)
    zs[0] = (dk[0] * SCALE).astype(BF)
    zs[1] = dv[0].astype(BF)
    send(zs, zr, dev_z, r_zb)

    arrived(xa.at[0], r_xa)
    xb[0] = (acc[xp_i, :, :, :QUART] + xa[0].astype(F32)).astype(BF)
    send(xb.at[0], xr.at[0], dev_xp, r_xr + 0)
    arrived(xa.at[1], r_xa + 1)
    xb[1] = (acc[xm_i, :, :, QUART:] + xa[1].astype(F32)).astype(BF)
    send(xb.at[1], xr.at[1], dev_xm, r_xr + 1)

    def back_own(n, _):
        back(lax.rem(n, 4), 1 + lax.div(n, 4))
        return 0

    lax.fori_loop(0, 8, back_own, 0)

    dqb[...] = (dq[...] * SCALE).astype(BF)
    r_dq, r_dk, r_dv = new("r", 4), new("r", 4), new("r", 4)

    def give(buf, out, r):
        local(buf.at[t_me], out.at[:, cols(t_me)], rsem.at[r + t_me])
        for n in (2, 3, 1):
            send(buf.at[peer_t[n]], out.at[:, cols(t_me)], peers[n], r + t_me)

    give(dqb, dq_o, r_dq)

    for n in range(4):
        arrived(xr.at[n], r_xr + n)
    rsum[:, :, :QUART] = acc[x, :, :, :QUART] + xr[0].astype(F32) + xr[3].astype(F32)
    rsum[:, :, QUART:] = acc[x, :, :, QUART:] + xr[1].astype(F32) + xr[2].astype(F32)
    y3s[...] = rsum[1 - yh].astype(BF)
    r_3 = new("r")
    send(y3s, y3r, dev_yi, r_3)

    arrived(cr, r_cb)
    arrived(yr, r_yb)
    arrived(zr, r_zb)
    for n, (own, fin_b, sc) in enumerate(((dk, dkb, SCALE), (dv, dvb, 1.0))):
        fin_b[0] = (own[1, :TILE] * sc).astype(BF)
        fin_b[1] = (own[1, TILE:] * sc + yr[n, :TILE].astype(F32)).astype(BF)
        fin_b[2] = (own[2, :TILE] * sc + zr[n, :TILE].astype(F32)).astype(BF)
        fin_b[3] = (
            own[2, TILE:] * sc + yr[n, TILE:].astype(F32) + zr[n, TILE:].astype(F32)
            + cr[n].astype(F32)
        ).astype(BF)
    give(dkb, dk_o, r_dk)
    give(dvb, dv_o, r_dv)

    arrived(y3r, r_3)
    half_o = pl.ds(pl.multiple_of((1 - ylo) * QUART, QUART), QUART)
    half_m = pl.ds(pl.multiple_of(ylo * QUART, QUART), QUART)
    y4s[...] = (rsum[yh, :, half_o] + y3r[:, half_o].astype(F32)).astype(BF)
    r_4 = new("r")
    send(y4s, y4r, dev_ylo, r_4)

    l_o = new("l", 6)

    def project(n):
        wide = pl.ds(n * 512, 512)
        oc[:, wide] = dot_nn(att[...], ws[:, :, wide].reshape(FEAT, 512)).astype(BF)
        local(oc.at[:, wide], out_o.at[:, wide], lsem.at[l_o + n])

    for n in range(3):
        project(n)
    arrived(y4r, r_4)
    z4s[...] = (rsum[yh, :, half_m] + y3r[:, half_m].astype(F32) + y4r[...].astype(F32)).astype(BF)
    r_z4 = new("r", 3)
    for n in (1, 2, 3):
        to = lax.rem(z + n, 4)
        some = pl.ds(pl.multiple_of(to * 16, 16), 16)
        send(z4s.at[some, pl.ds(0, QUART)], z4r.at[n - 1], (dp, to, wa), r_z4 + n - 1)
    for n in range(3, 6):
        project(n)
    mine = pl.ds(pl.multiple_of(z * 16, 16), 16)
    total = rsum[yh, mine, half_m] + y3r[mine, half_m].astype(F32) + y4r[mine, :].astype(F32)
    for n in range(3):
        arrived(z4r.at[n], r_z4 + n)
        total += z4r[n].astype(F32)
    fin[...] = total.astype(BF)
    place = wg_o.at[mine, pl.ds(pl.multiple_of(c * HALF + ylo * QUART, QUART), QUART)]
    r_f = new("r", 16)
    n = 0
    for a in range(4):
        for b in range(4):
            if a == 0 and b == 0:
                local(fin, place, rsem.at[r_f])
            else:
                dev = (dp, lax.rem(z + a, 4), lax.rem(wa + b, 4))
                send(fin, place, dev, r_f + n)
            n += 1

    for r, out in ((r_dq, dq_o), (r_dk, dk_o), (r_dv, dv_o)):
        for s in range(4):
            arrived(out.at[:, cols(s)], r + s)
    for n in range(6):
        wide = pl.ds(n * 512, 512)
        pltpu.make_async_copy(oc.at[:, wide], out_o.at[:, wide], lsem.at[l_o + n]).wait()
    for n in range(16):
        arrived(place, r_f + n)
    for copy in sends:
        copy.wait_send()
    assert counts["s"] <= N_SEND and counts["r"] <= N_RECV, counts


def on_device(q, k, v, g, w):
    def vm(*shape, dtype=BF):
        return pltpu.VMEM(shape, dtype)

    def f(*shape):
        return pltpu.VMEM(shape, F32)

    any_spec = pl.BlockSpec(memory_space=pl.ANY)
    tile = jax.ShapeDtypeStruct((TILE, FEAT), BF)
    outs = pl.pallas_call(
        kernel,
        out_shape=(
            jax.ShapeDtypeStruct((TILE, D), BF), tile, tile, tile,
            jax.ShapeDtypeStruct((64, D), BF),
        ),
        in_specs=[any_spec] * 5,
        out_specs=[any_spec] * 5,
        scratch_shapes=[
            vm(4, TILE, HD), vm(9, TILE, HD), vm(9, TILE, 2 * HD),
            f(12, TILE, 2 * TILE), f(TILE, TILE), f(4, TILE, HD),
            vm(12, TILE, 2 * TILE), vm(TILE, TILE), f(TILE, 2 * HD),
            f(4, TILE, HD), vm(4, TILE, HD), vm(4, TILE, HD), vm(4, TILE, HD), f(4, TILE, HD),
            f(4, TILE, HD), f(4, 2 * TILE, HD), f(4, 2 * TILE, HD),
                vm(2, 2 * TILE, HD), vm(2, 2 * TILE, HD), vm(2, TILE, HD),
            vm(2, 2 * TILE, HD), vm(2, 2 * TILE, HD), vm(2, TILE, HD),
            vm(4, TILE, HD), vm(4, TILE, HD), vm(4, TILE, HD),
            vm(TILE, FEAT), vm(TILE, FEAT), f(TILE, FEAT),
            vm(TILE, D), vm(8, 64, D), vm(TILE, D),
            f(4, 2, 64, HALF), vm(4, 2, 64, HALF), vm(4, 2, 64, HALF), vm(4, 2, 64, HALF),
            vm(2, 2, 64, QUART), vm(2, 2, 64, QUART), vm(4, 2, 64, QUART),
            f(2, 64, HALF), vm(64, HALF), vm(64, HALF),
            vm(64, QUART), vm(64, QUART), vm(64, QUART), vm(3, 16, QUART), vm(16, QUART),
            pltpu.SemaphoreType.DMA((N_SEND,)),
            pltpu.SemaphoreType.DMA((N_RECV,)),
            pltpu.SemaphoreType.DMA((8,)),
        ],
        compiler_params=pltpu.CompilerParams(
            collective_id=0, has_side_effects=True, vmem_limit_bytes=60 << 20
        ),
        name="sublayer",
    )(
        q.reshape(TILE, FEAT), k.reshape(TILE, FEAT), v.reshape(TILE, FEAT), g.reshape(TILE, D), w
    )
    outcome, dq, dk, dv, wg = outs
    return (
        outcome.reshape(g.shape),
        dq.astype(F32).reshape(q.shape),
        dk.astype(F32).reshape(q.shape),
        dv.astype(F32).reshape(q.shape),
        wg.astype(F32),
    )


def solution(mesh):
    tiles = P("dp", "ha", "wa", None, None)
    return jax.shard_map(
        on_device,
        mesh=mesh,
        in_specs=(tiles, tiles, tiles, tiles, P("dp", None)),
        out_specs=(tiles, tiles, tiles, tiles, P("dp", None)),
        check_vma=False,
    )
```

time: 483 us -> 92.1 us (0.19); the launches traced: 475 us -> 91.9 us
  waiting for transfers between devices: 164 us -> 0 us
  other arithmetic: 114 us -> 5.4 us
  local copies, waits for them, and re-layouts: 87.8 us -> 1.42 us
  Pallas kernels: 0 us -> 84.5 us
  matrix products: 58.6 us -> 0 us
  between operations: 26.1 us -> 0.67 us
  starting transfers between devices: 25.1 us -> 0 us
    psum x1 -> x0, waiting for transfers between devices: 87 us -> none  [on_device(): summed = lax.psum(local_term, ('dp', 'ha', 'wa'))]
    pallas_call x0 -> x1, Pallas kernels: none -> 84.5 us  [on_device(): pl.pallas_call(kernel, out_shape=(jax.ShapeDtypeStruct((TILE, D), BF), ti...]
    ppermute x8 -> x0, waiting for transfers between devices: 76.8 us -> none  [the longest x4 43.5 us: shifted(): lax.ppermute(value, axis, [(source, source + steps) for source in range(f...]
    dot_general x9 -> x0, matrix products: 58.6 us -> none  [the longest x6 46.1 us: product(): jnp.einsum(pattern, first_op, second_op, preferred_element_type=jnp.float32)]
    another operation x12 -> x0, other arithmetic: 57.5 us -> none  [the longest x6 20.7 us: spread_window(): return jnp.stack(spread_rows)]
    add x3 -> x0, other arithmetic: 25.2 us -> none  [the longest x1 18.2 us: on_device(): padded_grad = placed if padded_grad is None else padded_grad + placed]
    ppermute x8 -> x0, starting transfers between devices: 25.1 us -> none  [the longest x4 12.2 us: shifted(): lax.ppermute(value, axis, [(source, source + steps) for source in range(f...]
    another operation x6 -> x0, local copies, waits for them, and re-layouts: 22.5 us -> none
  transfers between devices with their start and end apart: 10 -> 0, of which waited for: 7 -> 0; matrix products, arithmetic and copies ran while one was open for 19% -> 0% of each run, Pallas kernels for 0% -> 0%
where the time goes in v1:
time: 92.1 us; the launch traced here: 91.9 us
  Pallas kernels  84.5 us (92%)
  other arithmetic  5.4 us (6%)
  local copies, waits for them, and re-layouts  1.42 us (2%)
    pallas_call x1, Pallas kernels, on_device(): pl.pallas_call(kernel, out_shape=(jax.ShapeDtypeStruct((TILE, D), BF), ti...  84.5 us
    reshape x1, other arithmetic, on_device(): dq.astype(F32).reshape(q.shape)  2.12 us
    convert_element_type x1, other arithmetic, on_device(): wg.astype(F32)  1.93 us

profile of v1, /device:TPU:1, one launch (start us, length us, event | category | flops | bytes accessed | tf_op | source)
XLA Modules:
  0.0 91.9 jit_solution(10490556256358913086)
XLA Ops:
  0.6 84.5 %sublayer.1 = (bf16[384,3072]{1,0:T(8,128)(2,1)}, bf16[384,512]{1,0:T(8,128)(2,1)}, bf16[384,512]{1,0:T(8,128)(2,1)}, bf16[384,512]{1,0:T(8,128)(2,1)}, bf16[64,3072]{1,0:T(8,128)(2,1)}) custom-call(bf16[384,512]{1,0:T(8,128)(2,1)} %bitcast.16, bf16[384,512]{1,0:T(8,128)(2,1)} %bitcast.17, bf16[384,512]{1,0:T(8,128)(2,1)} %bitcast.18, ...), custom_call_target="tpu_custom_call" | custom-call | tf_op jit(solution)/shard_map/sublayer/pallas_call | solution.py:475
  85.1 0.0 copy-start.1
  85.1 0.0 copy-start.2
  85.1 0.0 copy-start
  85.1 2.1 %bitcast_convert_fusion.2 = f32[1,1,1,384,512]{4,3,2,1,0:T(8,128)} fusion(bf16[384,512]{1,0:T(8,128)(2,1)} %get-tuple-element.11), kind=kLoop, calls=%fused_computation.2 | loop fusion | flops 196608 | bytes 1179648 | tf_op jit(solution)/shard_map/reshape | solution.py:512
  87.2 1.9 %convert_element_type.2 = f32[64,3072]{1,0:T(8,128)} convert(bf16[64,3072]{1,0:T(8,128)(2,1)} %get-tuple-element.14) | non-fusion elementwise | flops 196608 | bytes 1179648 | tf_op jit(solution)/shard_map/convert_element_type | solution.py:515
  89.2 0.0 copy-done.1
  89.2 0.0 copy-done.2
  89.2 1.4 %bitcast_convert_fusion = (f32[1,1,1,384,512]{4,3,2,1,0:T(8,128)}, f32[1,1,1,384,512]{4,3,2,1,0:T(8,128)}) fusion(bf16[384,512]{1,0:T(8,128)(2,1)S(1)} %copy-done.2, bf16[384,512]{1,0:T(8,128)(2,1)S(1)} %copy-done.1), kind=kLoop, calls=%fused_computation | loop fusion | flops 393216 | bytes 2359296 | tf_op jit(solution)/shard_map/reshape | solution.py:514
  90.5 0.0 copy-done
  90.5 1.4 %copy.11 = bf16[1,1,1,384,3072]{4,3,2,1,0:T(8,128)(2,1)} copy(bf16[1,1,1,384,3072]{4,3,2,1,0:T(8,128)(2,1)S(1)} %bitcast.14) | data formatting | bytes 4718592
Async XLA Ops:
  85.1 4.1 %copy-start.1 = (bf16[384,512]{1,0:T(8,128)(2,1)S(1)}, bf16[384,512]{1,0:T(8,128)(2,1)}, u32[]{:S(2)}) copy-start(bf16[384,512]{1,0:T(8,128)(2,1)} %get-tuple-element.12) | copy-start | bytes 1179652
  85.1 4.1 %copy-start.2 = (bf16[384,512]{1,0:T(8,128)(2,1)S(1)}, bf16[384,512]{1,0:T(8,128)(2,1)}, u32[]{:S(2)}) copy-start(bf16[384,512]{1,0:T(8,128)(2,1)} %get-tuple-element.13) | copy-start | bytes 1179652
  85.1 5.4 %copy-start = (bf16[384,3072]{1,0:T(8,128)(2,1)S(1)}, bf16[384,3072]{1,0:T(8,128)(2,1)}, u32[]{:S(2)}) copy-start(bf16[384,3072]{1,0:T(8,128)(2,1)} %get-tuple-element.10) | copy-start | bytes 7077892

commit v2 on v1

v2 whole, which is shorter than its diff:
```python
import math

import jax
import jax.numpy as jnp
from jax import lax
from jax.experimental import pallas as pl
from jax.experimental.pallas import tpu as pltpu
from jax.sharding import PartitionSpec as P

MESH = pl.DeviceIdType.MESH
BF = jnp.bfloat16
F32 = jnp.float32

TILE, HD, FEAT, D = 384, 128, 512, 3072
HALF, QUART = D // 2, D // 4
SCALE = HD**-0.5
EXP_SCALE = SCALE * math.log2(math.e)


def dot_nn(a, b):
    return lax.dot_general(a, b, (((1,), (0,)), ((), ())), preferred_element_type=F32)


def dot_nt(a, b):
    return lax.dot_general(a, b, (((1,), (1,)), ((), ())), preferred_element_type=F32)


def dot_tn(a, b):
    return lax.dot_general(a, b, (((0,), (0,)), ((), ())), preferred_element_type=F32)


def flip(v):
    return v + 1 - 2 * lax.rem(v, 2)


def unit_index(t, b):
    return 3 * t + b - 1 - lax.rem(t, 2) * (1 - lax.div(t, 2))


N_SEND, N_RECV, N_LOCAL = 128, 128, 16


def kernel(
    q_in, k_in, v_in, g_in, w_in,
    out_o, dq_o, dk_o, dv_o, wg_o,
    qg, kg, vg, s_ref, sc_ref, m_ref, p_ref, pc_ref, o_acc, linv, ob, dog, dop, delta,
    dq, dk, dv, ys, zs, cs, yr, zr, cr, dqb, dkb, dvb, dqr, dkr, dvr, att, gat, gat_acc, gov, g2, ws, oc,
    acc, xs, xa, xb, xr, rsum, y3s, y3r, y4s, y4r, z4s, z4r, fin, wgr,
    ssem, rsem, lsem,
):
    dp, z, wa = lax.axis_index("dp"), lax.axis_index("ha"), lax.axis_index("wa")
    x, yh = lax.rem(dp, 4), lax.div(dp, 4)
    c, ylo = lax.rem(wa, 2), lax.div(wa, 2)
    i, j = lax.rem(lax.div(z + 1, 2), 2), lax.rem(lax.div(wa + 1, 2), 2)
    t_me = 2 * i + j
    zp, wp = flip(z), flip(wa)
    peers = {1: (dp, z, wp), 2: (dp, zp, wa), 3: (dp, zp, wp)}
    peer_t = {0: t_me, 1: 2 * i + 1 - j, 2: 2 * (1 - i) + j, 3: 2 * (1 - i) + 1 - j}
    dev_y, dev_z, dev_c = (dp, z, 3 - wa), (dp, 3 - z, wa), (dp, 3 - z, 3 - wa)
    xp_i, xm_i, x2_i = lax.rem(x + 1, 4), lax.rem(x + 3, 4), lax.rem(x + 2, 4)
    dev_xp, dev_xm = (yh * 4 + xp_i, z, wa), (yh * 4 + xm_i, z, wa)
    dev_yi = (lax.rem(dp + 4, 8), z, lax.rem(wa + 2, 4))
    dev_core = peers[1]
    dev_ylo = (dp, z, lax.rem(wa + 2, 4))
    clip_devs = [
        (dp, lax.rem(z + a, 4), lax.rem(wa + b, 4)) for a in range(4) for b in range(4) if a or b
    ]
    fl = 4 * (1 - yh)

    sends = []
    counts = {"s": 0, "r": 0, "l": 0}

    def new(kind, n=1):
        first = counts[kind]
        counts[kind] += n
        return first

    def send(src, dst, dev, r):
        copy = pltpu.make_async_remote_copy(
            src, dst, ssem.at[new("s")], rsem.at[r], device_id=dev, device_id_type=MESH
        )
        copy.start()
        sends.append(copy)

    def local(src, dst, sem):
        pltpu.make_async_copy(src, dst, sem).start()

    def arrived(dst, r):
        pltpu.make_async_copy(dst, dst, rsem.at[r]).wait()

    def cols(n, width=HD):
        return pl.ds(pl.multiple_of(n * width, width), width)

    barrier = pltpu.get_barrier_semaphore()
    neighbours = clip_devs + [dev_xp, dev_xm, dev_yi]
    for dev in neighbours:
        pl.semaphore_signal(barrier, inc=1, device_id=dev, device_id_type=MESH)

    l_g, l_w = new("l"), new("l")
    local(g_in, gov, lsem.at[l_g])
    l_h = new("l")
    local(g_in.at[:, pl.ds(pl.multiple_of(c * HALF, HALF), HALF)], g2.at[0], lsem.at[l_h])
    local(w_in, ws.at[dp], lsem.at[l_w])
    r_k, r_q, r_v = new("r", 4), new("r", 4), new("r", 4)
    local(k_in.at[:, cols(t_me)], kg.at[2 + t_me], rsem.at[r_k + t_me])
    local(q_in.at[:, cols(t_me)], qg.at[t_me], rsem.at[r_q + t_me])
    local(v_in.at[:, cols(t_me)], vg.at[2 + t_me, :, pl.ds(0, HD)], rsem.at[r_v + t_me])
    pl.semaphore_wait(barrier, len(neighbours))

    for n in (2, 3, 1):
        send(k_in.at[:, cols(peer_t[n])], kg.at[2 + t_me], peers[n], r_k + t_me)
    hc = pl.ds(pl.multiple_of(c * HALF, HALF), HALF)
    hca = pl.ds(pl.multiple_of(c * HALF, HALF), QUART)
    hcb = pl.ds(pl.multiple_of(c * HALF + QUART, QUART), QUART)
    hall = pl.ds(0, 64)
    r_w = new("r", 8)
    r_wc = new("r", 7)
    send(w_in.at[hall, hc], ws.at[dp, hall, hc], dev_xp, r_w + 0)
    send(w_in.at[hall, hc], ws.at[dp, hall, hc], dev_xm, r_w + 1)
    send(w_in.at[hall, hc], ws.at[dp, hall, hc], dev_yi, r_w + 2)
    for n in (2, 3, 1):
        send(q_in.at[:, cols(peer_t[n])], qg.at[t_me], peers[n], r_q + t_me)
    for n in (2, 3, 1):
        send(v_in.at[:, cols(peer_t[n])], vg.at[2 + t_me, :, pl.ds(0, HD)], peers[n], r_v + t_me)

    r_gx = new("r")
    hc_o = pl.ds(pl.multiple_of((1 - c) * HALF, HALF), HALF)
    send(g_in.at[:, hc_o], g2.at[1], dev_core, r_gx)

    def ones(s, _):
        vg[s, :, HD:] = jnp.ones((TILE, HD), BF)
        return 0

    lax.fori_loop(0, 9, ones, 0)
    m_ref[...] = jnp.full(m_ref.shape, -jnp.inf, F32)
    dq[...] = jnp.zeros(dq.shape, F32)
    dk[...] = jnp.zeros(dk.shape, F32)
    dv[...] = jnp.zeros(dv.shape, F32)
    o_acc[...] = jnp.zeros(o_acc.shape, F32)

    def halo_of(buf, r_own, width, r_halo):
        def at(s):
            return buf.at[s] if width is None else buf.at[s, :, pl.ds(0, width)]

        for s in (3, 5, 4, 2):
            arrived(at(s), r_own + s - 2)
            if s == 3:
                send(at(3), at(6), dev_y, r_halo + 2)
            if s == 5:
                send(at(5), at(7), dev_y, r_halo + 3)
                send(at(5), at(1), dev_z, r_halo + 1)
                send(at(5), at(8), dev_c, r_halo + 4)
            if s == 4:
                send(at(4), at(0), dev_z, r_halo + 0)

    def w_at(d, columns):
        return ws.at[d, hall, columns]

    d_xm, d_xp, d_x2 = yh * 4 + xm_i, yh * 4 + xp_i, yh * 4 + x2_i
    f_x, f_xm, f_xp, f_x2 = fl + x, fl + xm_i, fl + xp_i, fl + x2_i

    r_kh, r_vh = new("r", 5), new("r", 5)
    halo_of(kg, r_k, None, r_kh)

    arrived(w_at(d_xm, hc), r_w + 0)
    send(w_at(d_xm, hca), w_at(d_xm, hca), dev_xp, r_w + 3)
    send(w_at(d_xm, hc), w_at(d_xm, hc), dev_core, r_wc + 0)
    arrived(w_at(d_xp, hc), r_w + 1)
    send(w_at(d_xp, hcb), w_at(d_xp, hcb), dev_xm, r_w + 4)
    send(w_at(d_xp, hc), w_at(d_xp, hc), dev_core, r_wc + 1)
    arrived(w_at(f_x, hc), r_w + 2)
    send(w_at(f_x, hc), w_at(f_x, hc), dev_xp, r_w + 5)
    send(w_at(f_x, hc), w_at(f_x, hc), dev_xm, r_w + 6)
    send(w_at(f_x, hc), w_at(f_x, hc), dev_core, r_wc + 2)

    for s in range(4):
        arrived(qg.at[s], r_q + s)
    arrived(w_at(d_x2, hca), r_w + 3)
    arrived(w_at(d_x2, hcb), r_w + 4)
    send(w_at(d_x2, hc), w_at(d_x2, hc), dev_yi, r_w + 7)
    send(w_at(d_x2, hc), w_at(d_x2, hc), dev_core, r_wc + 3)

    def scores(t, b):
        s = dot_nt(qg[t], kg[pl.ds(2 * b, 2)].reshape(2 * TILE, HD))
        s_ref[unit_index(t, b)] = s
        m = m_ref[t]
        for n in range(6):
            m = jnp.maximum(m, s[:, n * HD : (n + 1) * HD])
        m_ref[t] = m

    def own_scores(n, _):
        scores(lax.div(n, 2), 1 + lax.rem(n, 2))
        return 0

    lax.fori_loop(0, 8, own_scores, 0)

    for s, r in ((0, 0), (1, 1), (6, 2), (7, 3), (8, 4)):
        arrived(kg.at[s], r_kh + r)

    def halo_scores(n, _):
        late = lax.div(n, 2)
        scores(jnp.where(late == 0, 1 + 2 * n, n), 3 - 3 * late)
        return 0

    lax.fori_loop(0, 4, halo_scores, 0)
    s = dot_nt(qg[3], kg[8])
    sc_ref[...] = s
    m_ref[3] = jnp.maximum(
        jnp.maximum(m_ref[3], s[:, :HD]), jnp.maximum(s[:, HD : 2 * HD], s[:, 2 * HD :])
    )

    halo_of(vg, r_v, HD, r_vh)

    arrived(w_at(f_xm, hc), r_w + 5)
    send(w_at(f_xm, hc), w_at(f_xm, hc), dev_core, r_wc + 4)
    arrived(w_at(f_xp, hc), r_w + 6)
    send(w_at(f_xp, hc), w_at(f_xp, hc), dev_core, r_wc + 5)

    def row_max(t, _):
        m = jnp.max(m_ref[t], axis=-1, keepdims=True) * EXP_SCALE
        m_ref[t] = jnp.broadcast_to(m, (TILE, HD))
        return 0

    lax.fori_loop(0, 4, row_max, 0)

    def weigh(t, b):
        u = unit_index(t, b)
        p = jnp.exp2(s_ref[u] * EXP_SCALE - m_ref[t][:, :1]).astype(BF)
        p_ref[u] = p
        o_acc[t] += dot_nn(p, vg[pl.ds(2 * b, 2)].reshape(2 * TILE, 2 * HD))

    def weigh_own(n, _):
        weigh(lax.div(n, 2), 1 + lax.rem(n, 2))
        return 0

    lax.fori_loop(0, 4, weigh_own, 0)
    arrived(w_at(f_x2, hc), r_w + 7)
    send(w_at(f_x2, hc), w_at(f_x2, hc), dev_core, r_wc + 6)
    lax.fori_loop(4, 6, weigh_own, 0)

    pltpu.make_async_copy(g_in, gov, lsem.at[l_g]).wait()
    pltpu.make_async_copy(w_in, ws.at[dp], lsem.at[l_w]).wait()
    for n, d in enumerate((d_xm, d_xp, f_x, d_x2, f_xm, f_xp, f_x2)):
        arrived(w_at(d, hc_o), r_wc + n)
    gat_acc[...] = jnp.zeros(gat_acc.shape, F32)

    def grad_block(n, _):
        wide = pl.ds(pl.multiple_of(n * 512, 512), 512)
        gat_acc[...] += dot_nt(gov[:, wide], ws[:, :, wide].reshape(FEAT, 512))
        return 0

    lax.fori_loop(0, 6, grad_block, 0)
    gat[...] = gat_acc[...].astype(BF)
    r_g = new("r", 4)
    for n in (2, 3, 1):
        send(gat.at[:, cols(peer_t[n])], dog.at[t_me], peers[n], r_g + t_me)
    local(gat.at[:, cols(t_me)], dog.at[t_me], rsem.at[r_g + t_me])

    lax.fori_loop(6, 8, weigh_own, 0)
    for s, r in ((0, 0), (1, 1), (6, 2), (7, 3), (8, 4)):
        arrived(vg.at[s, :, pl.ds(0, HD)], r_vh + r)

    def weigh_halo(n, _):
        late = lax.div(n, 2)
        weigh(jnp.where(late == 0, 1 + 2 * n, n), 3 - 3 * late)
        return 0

    lax.fori_loop(0, 4, weigh_halo, 0)
    p = jnp.exp2(sc_ref[...] * EXP_SCALE - m_ref[3][:, :1]).astype(BF)
    pc_ref[...] = p
    o_acc[3] += dot_nn(p, vg[8])

    r_o = new("r", 4)
    for n in (2, 3, 1, 0):
        t = peer_t[n]
        inverse = 1.0 / o_acc[t, :, HD:]
        linv[t] = inverse
        ob[t] = (o_acc[t, :, :HD] * inverse).astype(BF)
        if n:
            send(ob.at[t], att.at[0, :, cols(t_me)], peers[n], r_o + t_me)
        else:
            local(ob.at[t], att.at[0, :, cols(t_me)], rsem.at[r_o + t_me])

    for s in range(4):
        arrived(dog.at[s], r_g + s)

    def prepare(t, _):
        scaled = (dog[t].astype(F32) * linv[t]).astype(BF)
        dop[t] = scaled
        d = jnp.sum(ob[t].astype(F32) * scaled.astype(F32), axis=-1, keepdims=True)
        delta[t] = jnp.broadcast_to(d, (TILE, HD))
        return 0

    lax.fori_loop(0, 4, prepare, 0)

    def back(t, b):
        p = p_ref[unit_index(t, b)]
        keys = kg[pl.ds(2 * b, 2)].reshape(2 * TILE, HD)
        values = vg[pl.ds(2 * b, 2), :, :HD].reshape(2 * TILE, HD)
        dprob = dot_nt(dop[t], values)
        ds = (p.astype(F32) * (dprob - delta[t][:, :1])).astype(BF)
        dq[t] += dot_nn(ds, keys)
        dk[b] += dot_tn(ds, qg[t])
        dv[b] += dot_tn(p, dop[t])

    def back_y(n, _):
        back(1 + 2 * n, jnp.int32(3))
        return 0

    def back_z(n, _):
        back(2 + n, jnp.int32(0))
        return 0

    r_cb, r_yb, r_zb = new("r"), new("r"), new("r")
    p = pc_ref[...]
    dprob = dot_nt(dop[3], vg[8, :, :HD])
    ds = (p.astype(F32) * (dprob - delta[3][:, :1])).astype(BF)
    dq[3] += dot_nn(ds, kg[8])
    cs[0] = dot_tn(ds, qg[3]).astype(BF)
    cs[1] = dot_tn(p, dop[3]).astype(BF)
    send(cs, cr, dev_c, r_cb)

    lax.fori_loop(0, 2, back_y, 0)
    ys[0] = dk[3].astype(BF)
    ys[1] = dv[3].astype(BF)
    send(ys, yr, dev_y, r_yb)
    lax.fori_loop(0, 1, back_z, 0)

    for s in range(4):
        arrived(att.at[0, :, cols(s)], r_o + s)
    r_a = new("r")
    send(att.at[0], att.at[1], dev_core, r_a)

    lax.fori_loop(1, 2, back_z, 0)
    zs[0] = dk[0].astype(BF)
    zs[1] = dv[0].astype(BF)
    send(zs, zr, dev_z, r_zb)

    arrived(g2.at[1], r_gx)
    pltpu.make_async_copy(g_in.at[:, hc], g2.at[0], lsem.at[l_h]).wait()
    arrived(att.at[1], r_a)

    def term(n, _):
        wide = pl.ds(pl.multiple_of(n * 256, 256), 256)
        d = dot_tn(att[...].reshape(2 * TILE, FEAT), g2[:, :, wide].reshape(2 * TILE, 256))
        for h in range(2):
            for xx in range(4):
                part = d[h * 256 + xx * 64 :][:64]
                acc[xx, h, :, wide] = part
                xs[xx, h, :, wide] = part.astype(BF)
        return 0

    two, rows = pl.ds(0, 2), pl.ds(0, 64)
    eighth = QUART // 2
    r_xa, r_xr = new("r", 4), new("r", 8)

    def part_a(n):
        return pl.ds(n * QUART, eighth)

    def part_b(n):
        return pl.ds(n * QUART + eighth, eighth)

    def x_first(n):
        send(xs.at[x2_i, two, rows, part_a(n)], xa.at[n, 0], dev_xp, r_xa + 2 * n)
        send(xs.at[x2_i, two, rows, part_b(n)], xa.at[n, 1], dev_xm, r_xa + 2 * n + 1)

    def x_plain(n):
        send(xs.at[xp_i, two, rows, part_b(n)], xr.at[n, 2], dev_xp, r_xr + 4 * n + 2)
        send(xs.at[xm_i, two, rows, part_a(n)], xr.at[n, 3], dev_xm, r_xr + 4 * n + 3)

    def x_second(n):
        arrived(xa.at[n, 0], r_xa + 2 * n)
        xb[n, 0] = (acc[xp_i, :, :, part_a(n)] + xa[n, 0].astype(F32)).astype(BF)
        send(xb.at[n, 0], xr.at[n, 0], dev_xp, r_xr + 4 * n)
        arrived(xa.at[n, 1], r_xa + 2 * n + 1)
        xb[n, 1] = (acc[xm_i, :, :, part_b(n)] + xa[n, 1].astype(F32)).astype(BF)
        send(xb.at[n, 1], xr.at[n, 1], dev_xm, r_xr + 4 * n + 1)

    r_y3, r_y4, r_z4, r_f = new("r", 2), new("r", 2), new("r", 6), new("r", 32)
    half_o = pl.ds(pl.multiple_of((1 - ylo) * eighth, eighth), eighth)
    half_m = pl.ds(pl.multiple_of(ylo * eighth, eighth), eighth)
    mine = pl.ds(pl.multiple_of(z * 16, 16), 16)

    def over_halves(n):
        for r in range(4):
            arrived(xr.at[n, r], r_xr + 4 * n + r)
        for h, (ring, plain) in enumerate(((0, 3), (1, 2))):
            here = pl.ds(h * eighth, eighth)
            there = pl.ds(n * QUART + h * eighth, eighth)
            rsum[n, :, :, here] = (
                acc[x, :, :, there] + xr[n, ring].astype(F32) + xr[n, plain].astype(F32)
            )
        y3s[n] = rsum[n, 1 - yh].astype(BF)
        send(y3s.at[n], y3r.at[n], dev_yi, r_y3 + n)

    def over_row(n):
        arrived(y3r.at[n], r_y3 + n)
        y4s[n] = (rsum[n, yh, :, half_o] + y3r[n, :, half_o].astype(F32)).astype(BF)
        send(y4s.at[n], y4r.at[n], dev_ylo, r_y4 + n)

    def over_rows(n):
        arrived(y4r.at[n], r_y4 + n)
        z4s[n] = (
            rsum[n, yh, :, half_m] + y3r[n, :, half_m].astype(F32) + y4r[n].astype(F32)
        ).astype(BF)
        for k in (1, 2, 3):
            to = lax.rem(z + k, 4)
            some = pl.ds(pl.multiple_of(to * 16, 16), 16)
            send(z4s.at[n, some, pl.ds(0, eighth)], z4r.at[n, k - 1], (dp, to, wa), r_z4 + 3 * n + k - 1)

    places = [
        wgr.at[mine, pl.ds(pl.multiple_of(c * HALF + n * QUART + ylo * eighth, eighth), eighth)]
        for n in range(2)
    ]

    def spread(n):
        total = rsum[n, yh, mine, half_m] + y3r[n, mine, half_m].astype(F32) + y4r[n, mine, :].astype(F32)
        for k in range(3):
            arrived(z4r.at[n, k], r_z4 + 3 * n + k)
            total += z4r[n, k].astype(F32)
        fin[n] = total.astype(BF)
        for k in range(16):
            if k == 0:
                local(fin.at[n], places[n], rsem.at[r_f + 16 * n])
            else:
                dev = (dp, lax.rem(z + k // 4, 4), lax.rem(wa + k % 4, 4))
                send(fin.at[n], places[n], dev, r_f + 16 * n + k)

    lax.fori_loop(0, 3, term, 0)
    x_first(0)
    x_plain(0)
    lax.fori_loop(3, 6, term, 0)
    x_first(1)

    r_dq, r_dk, r_dv = new("r", 4), new("r", 4), new("r", 4)
    b_far, b_near = 2 - i, 1 + i

    def back_far(n, _):
        back(n, b_far)
        return 0

    def give(buf, into, r, n):
        if n:
            send(buf.at[peer_t[n]], into.at[:, cols(t_me)], peers[n], r + t_me)
        else:
            local(buf.at[t_me], into.at[:, cols(t_me)], rsem.at[r + t_me])

    def close_keys(b, order):
        for own, buf, sc in ((dk, dkb, SCALE), (dv, dvb, 1.0)):
            buf[pl.ds(2 * (b - 1), 2)] = (own[b] * sc).astype(BF).reshape(2, TILE, HD)
        for n in order:
            give(dkb, dkr, r_dk, n)
            give(dvb, dvr, r_dv, n)

    def near(n):
        t = peer_t[n]
        back(t, b_near)
        dqb[t] = (dq[t] * SCALE).astype(BF)
        give(dqb, dqr, r_dq, n)

    l_o, l_d = new("l", 6), new("l", 4)

    def project(n):
        wide = pl.ds(n * 512, 512)
        oc[:, wide] = dot_nn(att[0], ws[:, :, wide].reshape(FEAT, 512)).astype(BF)
        local(oc.at[:, wide], out_o.at[:, wide], lsem.at[l_o + n])

    lax.fori_loop(0, 3, back_far, 0)
    x_second(0)
    x_plain(1)
    lax.fori_loop(3, 4, back_far, 0)
    near(2)
    x_second(1)
    near(3)
    over_halves(0)

    arrived(cr, r_cb)
    arrived(yr, r_yb)
    arrived(zr, r_zb)
    for n, own in enumerate((dk, dv)):
        own[1, TILE:] += yr[n, :TILE].astype(F32)
        own[2, :TILE] += zr[n, :TILE].astype(F32)
        own[2, TILE:] += (yr[n, TILE:].astype(F32) + zr[n, TILE:].astype(F32)) + cr[n].astype(F32)
    close_keys(b_far, (2, 3))
    near(1)
    over_row(0)
    over_halves(1)
    near(0)
    over_rows(0)
    close_keys(b_near, (1, 0))
    over_row(1)
    project(0)
    spread(0)
    project(1)
    over_rows(1)
    project(2)
    project(3)
    spread(1)
    project(4)
    project(5)

    for n, (r, got) in enumerate(((r_dq, dqr), (r_dk, dkr), (r_dv, dvr))):
        for s in range(4):
            arrived(got.at[:, cols(s)], r + s)
        local(got, (dq_o, dk_o, dv_o)[n], lsem.at[l_d + n])

    for n in range(2):
        for k in range(16):
            arrived(places[n], r_f + 16 * n + k)
    local(wgr, wg_o, lsem.at[l_d + 3])
    for n in range(6):
        wide = pl.ds(n * 512, 512)
        pltpu.make_async_copy(oc.at[:, wide], out_o.at[:, wide], lsem.at[l_o + n]).wait()
    for copy in sends:
        copy.wait_send()
    for n, (got, out) in enumerate(((dqr, dq_o), (dkr, dk_o), (dvr, dv_o), (wgr, wg_o))):
        pltpu.make_async_copy(got, out, lsem.at[l_d + n]).wait()
    assert counts["s"] <= N_SEND and counts["r"] <= N_RECV and counts["l"] <= N_LOCAL, counts


def widen(oi, qi, ki, vi, wi, oo, qo, ko, vo, wo, ov, qv, kv, vv, wv, qf, kf, vf, wf, isem, osem):
    top, low = pl.ds(0, TILE // 2), pl.ds(TILE // 2, TILE // 2)
    halves = [(oi.at[h], ov.at[h], oo.at[h]) for h in (top, low)]
    sets = ((qi, qv, qf, qo), (ki, kv, kf, ko), (vi, vv, vf, vo), (wi, wv, wf, wo))
    for n, (src, mid, _, _) in enumerate(sets):
        pltpu.make_async_copy(src, mid, isem.at[n]).start()
    for n, (src, mid, _) in enumerate(halves):
        pltpu.make_async_copy(src, mid, isem.at[4 + n]).start()
    for n, (src, mid, wide, out) in enumerate(sets):
        pltpu.make_async_copy(src, mid, isem.at[n]).wait()
        wide[...] = mid[...].astype(F32)
        pltpu.make_async_copy(wide, out, osem.at[n]).start()
    for n, (src, mid, out) in enumerate(halves):
        pltpu.make_async_copy(src, mid, isem.at[4 + n]).wait()
        pltpu.make_async_copy(mid, out, osem.at[4 + n]).start()
    for n, (_, _, wide, out) in enumerate(sets):
        pltpu.make_async_copy(wide, out, osem.at[n]).wait()
    for n, (_, mid, out) in enumerate(halves):
        pltpu.make_async_copy(mid, out, osem.at[4 + n]).wait()


def on_device(q, k, v, g, w):
    def vm(*shape, dtype=BF):
        return pltpu.VMEM(shape, dtype)

    def f(*shape):
        return pltpu.VMEM(shape, F32)

    any_spec = pl.BlockSpec(memory_space=pl.ANY)
    tile = jax.ShapeDtypeStruct((TILE, FEAT), BF)
    outs = pl.pallas_call(
        kernel,
        out_shape=(
            jax.ShapeDtypeStruct((TILE, D), BF),
            *[jax.ShapeDtypeStruct((TILE, FEAT), BF)] * 3,
            jax.ShapeDtypeStruct((64, D), BF),
        ),
        in_specs=[any_spec] * 5,
        out_specs=[any_spec] * 5,
        scratch_shapes=[
            vm(4, TILE, HD), vm(9, TILE, HD), vm(9, TILE, 2 * HD),
            f(12, TILE, 2 * TILE), f(TILE, TILE), f(4, TILE, HD),
            vm(12, TILE, 2 * TILE), vm(TILE, TILE), f(4, TILE, 2 * HD),
            f(4, TILE, HD), vm(4, TILE, HD), vm(4, TILE, HD), vm(4, TILE, HD), f(4, TILE, HD),
            f(4, TILE, HD), f(4, 2 * TILE, HD), f(4, 2 * TILE, HD),
            vm(2, 2 * TILE, HD), vm(2, 2 * TILE, HD), vm(2, TILE, HD),
            vm(2, 2 * TILE, HD), vm(2, 2 * TILE, HD), vm(2, TILE, HD),
            vm(4, TILE, HD), vm(4, TILE, HD), vm(4, TILE, HD),
            vm(TILE, FEAT), vm(TILE, FEAT), vm(TILE, FEAT),
            vm(2, TILE, FEAT), vm(TILE, FEAT), f(TILE, FEAT),
            vm(TILE, D), vm(2, TILE, HALF), vm(8, 64, D), vm(TILE, D),
            f(4, 2, 64, HALF), vm(4, 2, 64, HALF),
            vm(2, 2, 2, 64, QUART // 2), vm(2, 2, 2, 64, QUART // 2), vm(2, 4, 2, 64, QUART // 2),
            f(2, 2, 64, QUART), vm(2, 64, QUART), vm(2, 64, QUART),
            vm(2, 64, QUART // 2), vm(2, 64, QUART // 2), vm(2, 64, QUART // 2),
            vm(2, 3, 16, QUART // 2), vm(2, 16, QUART // 2), vm(64, D),
            pltpu.SemaphoreType.DMA((N_SEND,)),
            pltpu.SemaphoreType.DMA((N_RECV,)),
            pltpu.SemaphoreType.DMA((N_LOCAL,)),
        ],
        compiler_params=pltpu.CompilerParams(
            collective_id=0, has_side_effects=True, vmem_limit_bytes=62 << 20
        ),
        name="sublayer",
    )(
        q.reshape(TILE, FEAT), k.reshape(TILE, FEAT), v.reshape(TILE, FEAT), g.reshape(TILE, D), w
    )
    outcome, dq, dk, dv, wg = pl.pallas_call(
        widen,
        out_shape=(
            jax.ShapeDtypeStruct((TILE, D), BF),
            *[jax.ShapeDtypeStruct((TILE, FEAT), F32)] * 3,
            jax.ShapeDtypeStruct((64, D), F32),
        ),
        in_specs=[any_spec] * 5,
        out_specs=[any_spec] * 5,
        scratch_shapes=[
            vm(TILE, D), *[vm(TILE, FEAT)] * 3, vm(64, D), *[f(TILE, FEAT)] * 3, f(64, D),
            pltpu.SemaphoreType.DMA((6,)), pltpu.SemaphoreType.DMA((6,)),
        ],
        compiler_params=pltpu.CompilerParams(vmem_limit_bytes=24 << 20),
        name="widen",
    )(*outs)
    return (
        outcome.reshape(g.shape), dq.reshape(q.shape), dk.reshape(q.shape), dv.reshape(q.shape), wg
    )


def solution(mesh):
    tiles = P("dp", "ha", "wa", None, None)
    return jax.shard_map(
        on_device,
        mesh=mesh,
        in_specs=(tiles, tiles, tiles, tiles, P("dp", None)),
        out_specs=(tiles, tiles, tiles, tiles, P("dp", None)),
        check_vma=False,
    )
```

time: 92.1 us -> 89.5 us (0.972)
  other arithmetic: 5.4 us -> 0 us
  local copies, waits for them, and re-layouts: 1.42 us -> 5.64 us
  Pallas kernels: 84.5 us -> 82.7 us
    unnamed x7 -> x10, local copies, waits for them, and re-layouts: 1.42 us -> 5.64 us
    reshape x2 -> x0, other arithmetic: 3.48 us -> none  [the longest x1 2.12 us: on_device(): dq.astype(F32).reshape(q.shape)]
    convert_element_type x1 -> x0, other arithmetic: 1.93 us -> none  [on_device(): wg.astype(F32)]
    pallas_call x1 -> x2, Pallas kernels: 84.5 us -> 82.7 us  [the longest x1 78.9 us: on_device(): pl.pallas_call(kernel, out_shape=(jax.ShapeDtypeStruct((TILE, D), BF), *[...]
where the time goes in v2:
time: 89.5 us; the launch traced here: 89.2 us
  Pallas kernels  82.7 us (92%)
  local copies, waits for them, and re-layouts  5.64 us (6%)
    pallas_call x1, Pallas kernels, on_device(): pl.pallas_call(kernel, out_shape=(jax.ShapeDtypeStruct((TILE, D), BF), *[...  78.9 us
    unnamed x10, local copies, waits for them, and re-layouts  5.64 us
    pallas_call x1, Pallas kernels, on_device(): pl.pallas_call(widen, out_shape=(jax.ShapeDtypeStruct((TILE, D), BF), *[j...  3.81 us

profile of v2, /device:TPU:1, one launch (start us, length us, event | category | flops | bytes accessed | tf_op | source)
XLA Modules:
  0.0 89.2 jit_solution(7119838604717104482)
XLA Ops:
  0.6 78.9 %sublayer.1 = (bf16[384,3072]{1,0:T(8,128)(2,1)}, bf16[384,512]{1,0:T(8,128)(2,1)}, bf16[384,512]{1,0:T(8,128)(2,1)}, bf16[384,512]{1,0:T(8,128)(2,1)}, bf16[64,3072]{1,0:T(8,128)(2,1)}) custom-call(bf16[384,512]{1,0:T(8,128)(2,1)} %bitcast.9, bf16[384,512]{1,0:T(8,128)(2,1)} %bitcast.10, bf16[384,512]{1,0:T(8,128)(2,1)} %bitcast.11, ...), custom_call_target="tpu_custom_call" | custom-call | tf_op jit(solution)/shard_map/sublayer/pallas_call | solution.py:551
  79.5 0.0 copy-start
  79.5 1.7 %copy-done = bf16[384,3072]{1,0:T(8,128)(2,1)S(1)} copy-done((bf16[384,3072]{1,0:T(8,128)(2,1)S(1)}, bf16[384,3072]{1,0:T(8,128)(2,1)}, u32[]{:S(2)}) %copy-start) | copy-done | bytes 2359320
  81.2 0.0 copy-start.1
  81.2 1.0 %copy-done.1 = bf16[384,512]{1,0:T(8,128)(2,1)S(1)} copy-done((bf16[384,512]{1,0:T(8,128)(2,1)S(1)}, bf16[384,512]{1,0:T(8,128)(2,1)}, u32[]{:S(2)}) %copy-start.1) | copy-done | bytes 393240
  82.2 0.0 copy-start.2
  82.2 1.0 %copy-done.2 = bf16[384,512]{1,0:T(8,128)(2,1)S(1)} copy-done((bf16[384,512]{1,0:T(8,128)(2,1)S(1)}, bf16[384,512]{1,0:T(8,128)(2,1)}, u32[]{:S(2)}) %copy-start.2) | copy-done | bytes 393240
  83.2 0.0 copy-start.3
  83.2 1.0 %copy-done.3 = bf16[384,512]{1,0:T(8,128)(2,1)S(1)} copy-done((bf16[384,512]{1,0:T(8,128)(2,1)S(1)}, bf16[384,512]{1,0:T(8,128)(2,1)}, u32[]{:S(2)}) %copy-start.3) | copy-done | bytes 393240
  84.2 0.0 copy-start.4
  84.2 1.0 %copy-done.4 = bf16[64,3072]{1,0:T(8,128)(2,1)S(1)} copy-done((bf16[64,3072]{1,0:T(8,128)(2,1)S(1)}, bf16[64,3072]{1,0:T(8,128)(2,1)}, u32[]{:S(2)}) %copy-start.4) | copy-done | bytes 393240
  85.2 3.8 %widen.1 = (bf16[384,3072]{1,0:T(8,128)(2,1)}, f32[384,512]{1,0:T(8,128)}, f32[384,512]{1,0:T(8,128)}, f32[384,512]{1,0:T(8,128)}, f32[64,3072]{1,0:T(8,128)}) custom-call(bf16[384,3072]{1,0:T(8,128)(2,1)S(1)} %copy-done, bf16[384,512]{1,0:T(8,128)(2,1)S(1)} %copy-done.1, bf16[384,512]{1,0:T(8,128)(2,1)S(1)} %copy-done.2, bf16[384,512]{1,0:T(8,128)(2,1)S(1)} %copy-done.3, ...), custom_call_target="tpu_custom_call" | custom-call | tf_op jit(solution)/shard_map/widen/pallas_call | solution.py:588
Async XLA Ops:
  79.5 1.7 %copy-start = (bf16[384,3072]{1,0:T(8,128)(2,1)S(1)}, bf16[384,3072]{1,0:T(8,128)(2,1)}, u32[]{:S(2)}) copy-start(bf16[384,3072]{1,0:T(8,128)(2,1)} %get-tuple-element.15.oi) | copy-start | bytes 7077892
  81.2 1.0 %copy-start.1 = (bf16[384,512]{1,0:T(8,128)(2,1)S(1)}, bf16[384,512]{1,0:T(8,128)(2,1)}, u32[]{:S(2)}) copy-start(bf16[384,512]{1,0:T(8,128)(2,1)} %get-tuple-element.16.qi) | copy-start | bytes 1179652
  82.2 1.0 %copy-start.2 = (bf16[384,512]{1,0:T(8,128)(2,1)S(1)}, bf16[384,512]{1,0:T(8,128)(2,1)}, u32[]{:S(2)}) copy-start(bf16[384,512]{1,0:T(8,128)(2,1)} %get-tuple-element.17.ki) | copy-start | bytes 1179652
  83.2 1.0 %copy-start.3 = (bf16[384,512]{1,0:T(8,128)(2,1)S(1)}, bf16[384,512]{1,0:T(8,128)(2,1)}, u32[]{:S(2)}) copy-start(bf16[384,512]{1,0:T(8,128)(2,1)} %get-tuple-element.18.vi) | copy-start | bytes 1179652
  84.2 1.0 %copy-start.4 = (bf16[64,3072]{1,0:T(8,128)(2,1)S(1)}, bf16[64,3072]{1,0:T(8,128)(2,1)}, u32[]{:S(2)}) copy-start(bf16[64,3072]{1,0:T(8,128)(2,1)} %get-tuple-element.19.wi) | copy-start | bytes 1179652

commit v3 on v2

--- a/solution.py
+++ b/solution.py
@@ -45,7 +45,7 @@
     out_o, dq_o, dk_o, dv_o, wg_o,
     qg, kg, vg, s_ref, sc_ref, m_ref, p_ref, pc_ref, o_acc, linv, ob, dog, dop, delta,
     dq, dk, dv, ys, zs, cs, yr, zr, cr, dqb, dkb, dvb, dqr, dkr, dvr, att, gat, gat_acc, gov, g2, ws, oc,
-    acc, xs, xa, xb, xr, rsum, y3s, y3r, y4s, y4r, z4s, z4r, fin, wgr,
+    acc, xs, xa, xb, xr, rsum, y3s, y3r, y4s, z4r, fin, wgr,
     ssem, rsem, lsem,
 ):
     dp, z, wa = lax.axis_index("dp"), lax.axis_index("ha"), lax.axis_index("wa")
@@ -311,19 +311,20 @@
         back(2 + n, jnp.int32(0))
         return 0
 
-    r_cb, r_yb, r_zb = new("r"), new("r"), new("r")
+    r_cb, r_yb, r_zb = new("r", 2), new("r", 2), new("r", 2)
     p = pc_ref[...]
     dprob = dot_nt(dop[3], vg[8, :, :HD])
     ds = (p.astype(F32) * (dprob - delta[3][:, :1])).astype(BF)
     dq[3] += dot_nn(ds, kg[8])
     cs[0] = dot_tn(ds, qg[3]).astype(BF)
     cs[1] = dot_tn(p, dop[3]).astype(BF)
-    send(cs, cr, dev_c, r_cb)
+    send(cs.at[0], cr.at[0], dev_c, r_cb)
 
     lax.fori_loop(0, 2, back_y, 0)
     ys[0] = dk[3].astype(BF)
     ys[1] = dv[3].astype(BF)
-    send(ys, yr, dev_y, r_yb)
+    for n in range(2):
+        send(ys.at[n], yr.at[n], dev_y, r_yb + n)
     lax.fori_loop(0, 1, back_z, 0)
 
     for s in range(4):
@@ -334,7 +335,9 @@
     lax.fori_loop(1, 2, back_z, 0)
     zs[0] = dk[0].astype(BF)
     zs[1] = dv[0].astype(BF)
-    send(zs, zr, dev_z, r_zb)
+    for n in range(2):
+        send(zs.at[n], zr.at[n], dev_z, r_zb + n)
+    send(cs.at[1], cr.at[1], dev_c, r_cb + 1)
 
     arrived(g2.at[1], r_gx)
     pltpu.make_async_copy(g_in.at[:, hc], g2.at[0], lsem.at[l_h]).wait()
@@ -376,8 +379,7 @@
         xb[n, 1] = (acc[xm_i, :, :, part_b(n)] + xa[n, 1].astype(F32)).astype(BF)
         send(xb.at[n, 1], xr.at[n, 1], dev_xm, r_xr + 4 * n + 1)
 
-    r_y3, r_y4, r_z4, r_f = new("r", 2), new("r", 2), new("r", 6), new("r", 32)
-    half_o = pl.ds(pl.multiple_of((1 - ylo) * eighth, eighth), eighth)
+    r_y3, r_z4, r_f = new("r", 2), new("r", 14), new("r", 32)
     half_m = pl.ds(pl.multiple_of(ylo * eighth, eighth), eighth)
     mine = pl.ds(pl.multiple_of(z * 16, 16), 16)
 
@@ -395,18 +397,12 @@
 
     def over_row(n):
         arrived(y3r.at[n], r_y3 + n)
-        y4s[n] = (rsum[n, yh, :, half_o] + y3r[n, :, half_o].astype(F32)).astype(BF)
-        send(y4s.at[n], y4r.at[n], dev_ylo, r_y4 + n)
-
-    def over_rows(n):
-        arrived(y4r.at[n], r_y4 + n)
-        z4s[n] = (
-            rsum[n, yh, :, half_m] + y3r[n, :, half_m].astype(F32) + y4r[n].astype(F32)
-        ).astype(BF)
-        for k in (1, 2, 3):
-            to = lax.rem(z + k, 4)
-            some = pl.ds(pl.multiple_of(to * 16, 16), 16)
-            send(z4s.at[n, some, pl.ds(0, eighth)], z4r.at[n, k - 1], (dp, to, wa), r_z4 + 3 * n + k - 1)
+        y4s[n] = (rsum[n, yh] + y3r[n].astype(F32)).astype(BF)
+        for k in range(1, 8):
+            to_z, to_y = lax.rem(z + k // 2, 4), lax.rem(ylo + k % 2, 2)
+            some = pl.ds(pl.multiple_of(to_z * 16, 16), 16)
+            part = pl.ds(pl.multiple_of(to_y * eighth, eighth), eighth)
+            send(y4s.at[n, some, part], z4r.at[n, k - 1], (dp, to_z, 2 * to_y + c), r_z4 + 7 * n + k - 1)
 
     places = [
         wgr.at[mine, pl.ds(pl.multiple_of(c * HALF + n * QUART + ylo * eighth, eighth), eighth)]
@@ -414,9 +410,9 @@
     ]
 
     def spread(n):
-        total = rsum[n, yh, mine, half_m] + y3r[n, mine, half_m].astype(F32) + y4r[n, mine, :].astype(F32)
-        for k in range(3):
-            arrived(z4r.at[n, k], r_z4 + 3 * n + k)
+        total = rsum[n, yh, mine, half_m] + y3r[n, mine, half_m].astype(F32)
+        for k in range(7):
+            arrived(z4r.at[n, k], r_z4 + 7 * n + k)
             total += z4r[n, k].astype(F32)
         fin[n] = total.astype(BF)
         for k in range(16):
@@ -445,12 +441,19 @@
         else:
             local(buf.at[t_me], into.at[:, cols(t_me)], rsem.at[r + t_me])
 
-    def close_keys(b, order):
-        for own, buf, sc in ((dk, dkb, SCALE), (dv, dvb, 1.0)):
-            buf[pl.ds(2 * (b - 1), 2)] = (own[b] * sc).astype(BF).reshape(2, TILE, HD)
-        for n in order:
-            give(dkb, dkr, r_dk, n)
-            give(dvb, dvr, r_dv, n)
+    def add_neighbours(n):
+        own = (dk, dv)[n]
+        for buf, r in ((cr, r_cb), (yr, r_yb), (zr, r_zb)):
+            arrived(buf.at[n], r + n)
+        own[1, TILE:] += yr[n, :TILE].astype(F32)
+        own[2, :TILE] += zr[n, :TILE].astype(F32)
+        own[2, TILE:] += (yr[n, TILE:].astype(F32) + zr[n, TILE:].astype(F32)) + cr[n].astype(F32)
+
+    def close_keys(n, b, order):
+        own, buf, into, r, sc = ((dk, dkb, dkr, r_dk, SCALE), (dv, dvb, dvr, r_dv, 1.0))[n]
+        buf[pl.ds(2 * (b - 1), 2)] = (own[b] * sc).astype(BF).reshape(2, TILE, HD)
+        for k in order:
+            give(buf, into, r, k)
 
     def near(n):
         t = peer_t[n]
@@ -471,33 +474,24 @@
     lax.fori_loop(3, 4, back_far, 0)
     near(2)
     x_second(1)
+    add_neighbours(0)
+    close_keys(0, b_far, (2, 3))
     near(3)
     over_halves(0)
-
-    arrived(cr, r_cb)
-    arrived(yr, r_yb)
-    arrived(zr, r_zb)
-    for n, own in enumerate((dk, dv)):
-        own[1, TILE:] += yr[n, :TILE].astype(F32)
-        own[2, :TILE] += zr[n, :TILE].astype(F32)
-        own[2, TILE:] += (yr[n, TILE:].astype(F32) + zr[n, TILE:].astype(F32)) + cr[n].astype(F32)
-    close_keys(b_far, (2, 3))
     near(1)
+    add_neighbours(1)
+    close_keys(1, b_far, (2, 3))
     over_row(0)
     over_halves(1)
     near(0)
-    over_rows(0)
-    close_keys(b_near, (1, 0))
+    close_keys(0, b_near, (1, 0))
+    close_keys(1, b_near, (1, 0))
+    spread(0)
+    project(0)
     over_row(1)
-    project(0)
-    spread(0)
-    project(1)
-    over_rows(1)
-    project(2)
-    project(3)
+    for n in range(1, 6):
+        project(n)
     spread(1)
-    project(4)
-    project(5)
 
     for n, (r, got) in enumerate(((r_dq, dqr), (r_dk, dkr), (r_dv, dvr))):
         for s in range(4):
@@ -572,8 +566,8 @@
             f(4, 2, 64, HALF), vm(4, 2, 64, HALF),
             vm(2, 2, 2, 64, QUART // 2), vm(2, 2, 2, 64, QUART // 2), vm(2, 4, 2, 64, QUART // 2),
             f(2, 2, 64, QUART), vm(2, 64, QUART), vm(2, 64, QUART),
-            vm(2, 64, QUART // 2), vm(2, 64, QUART // 2), vm(2, 64, QUART // 2),
-            vm(2, 3, 16, QUART // 2), vm(2, 16, QUART // 2), vm(64, D),
+            vm(2, 64, QUART),
+            vm(2, 7, 16, QUART // 2), vm(2, 16, QUART // 2), vm(64, D),
             pltpu.SemaphoreType.DMA((N_SEND,)),
             pltpu.SemaphoreType.DMA((N_RECV,)),
             pltpu.SemaphoreType.DMA((N_LOCAL,)),
@@ -598,7 +592,7 @@
             vm(TILE, D), *[vm(TILE, FEAT)] * 3, vm(64, D), *[f(TILE, FEAT)] * 3, f(64, D),
             pltpu.SemaphoreType.DMA((6,)), pltpu.SemaphoreType.DMA((6,)),
         ],
-        compiler_params=pltpu.CompilerParams(vmem_limit_bytes=24 << 20),
+        compiler_params=pltpu.CompilerParams(vmem_limit_bytes=62 << 20),
         name="widen",
     )(*outs)
     return (

time: 89.5 us -> 84.1 us (0.940)
  local copies, waits for them, and re-layouts: 5.64 us -> 0 us
    unnamed x10 -> x0, local copies, waits for them, and re-layouts: 5.64 us -> none
where the time goes in v3:
time: 84.1 us; the launch traced here: 84 us
  Pallas kernels  83.2 us (99%)
    pallas_call x1, Pallas kernels, on_device(): pl.pallas_call(kernel, out_shape=(jax.ShapeDtypeStruct((TILE, D), BF), *[...  79.6 us
    pallas_call x1, Pallas kernels, on_device(): pl.pallas_call(widen, out_shape=(jax.ShapeDtypeStruct((TILE, D), BF), *[j...  3.59 us

profile of v3, /device:TPU:1, one launch (start us, length us, event | category | flops | bytes accessed | tf_op | source)
XLA Modules:
  0.0 84.0 jit_solution(3206019132906301819)
XLA Ops:
  0.6 79.6 %sublayer.1 = (bf16[384,3072]{1,0:T(8,128)(2,1)}, bf16[384,512]{1,0:T(8,128)(2,1)}, bf16[384,512]{1,0:T(8,128)(2,1)}, bf16[384,512]{1,0:T(8,128)(2,1)}, bf16[64,3072]{1,0:T(8,128)(2,1)}) custom-call(bf16[384,512]{1,0:T(8,128)(2,1)} %bitcast.9, bf16[384,512]{1,0:T(8,128)(2,1)} %bitcast.10, bf16[384,512]{1,0:T(8,128)(2,1)} %bitcast.11, ...), custom_call_target="tpu_custom_call" | custom-call | tf_op jit(solution)/shard_map/sublayer/pallas_call | solution.py:545
  80.2 3.6 %widen.1 = (bf16[384,3072]{1,0:T(8,128)(2,1)}, f32[384,512]{1,0:T(8,128)}, f32[384,512]{1,0:T(8,128)}, f32[384,512]{1,0:T(8,128)}, f32[64,3072]{1,0:T(8,128)}) custom-call(bf16[384,3072]{1,0:T(8,128)(2,1)} %get-tuple-element.15.oi, bf16[384,512]{1,0:T(8,128)(2,1)} %get-tuple-element.16.qi, bf16[384,512]{1,0:T(8,128)(2,1)} %get-tuple-element.17.ki, ...), custom_call_target="tpu_custom_call" | custom-call | tf_op jit(solution)/shard_map/widen/pallas_call | solution.py:582

commit v4 on v3

--- a/solution.py
+++ b/solution.py
@@ -332,12 +332,6 @@
     r_a = new("r")
     send(att.at[0], att.at[1], dev_core, r_a)
 
-    lax.fori_loop(1, 2, back_z, 0)
-    zs[0] = dk[0].astype(BF)
-    zs[1] = dv[0].astype(BF)
-    for n in range(2):
-        send(zs.at[n], zr.at[n], dev_z, r_zb + n)
-    send(cs.at[1], cr.at[1], dev_c, r_cb + 1)
 
     arrived(g2.at[1], r_gx)
     pltpu.make_async_copy(g_in.at[:, hc], g2.at[0], lsem.at[l_h]).wait()
@@ -428,6 +422,13 @@
     lax.fori_loop(3, 6, term, 0)
     x_first(1)
 
+    lax.fori_loop(1, 2, back_z, 0)
+    zs[0] = dk[0].astype(BF)
+    zs[1] = dv[0].astype(BF)
+    for n in range(2):
+        send(zs.at[n], zr.at[n], dev_z, r_zb + n)
+    send(cs.at[1], cr.at[1], dev_c, r_cb + 1)
+
     r_dq, r_dk, r_dv = new("r", 4), new("r", 4), new("r", 4)
     b_far, b_near = 2 - i, 1 + i
 
@@ -468,30 +469,29 @@
         oc[:, wide] = dot_nn(att[0], ws[:, :, wide].reshape(FEAT, 512)).astype(BF)
         local(oc.at[:, wide], out_o.at[:, wide], lsem.at[l_o + n])
 
-    lax.fori_loop(0, 3, back_far, 0)
+    lax.fori_loop(0, 2, back_far, 0)
     x_second(0)
     x_plain(1)
-    lax.fori_loop(3, 4, back_far, 0)
+    lax.fori_loop(2, 4, back_far, 0)
+    x_second(1)
     near(2)
-    x_second(1)
+    over_halves(0)
+    near(3)
     add_neighbours(0)
     close_keys(0, b_far, (2, 3))
-    near(3)
-    over_halves(0)
     near(1)
+    over_row(0)
+    over_halves(1)
     add_neighbours(1)
     close_keys(1, b_far, (2, 3))
-    over_row(0)
-    over_halves(1)
+    spread(0)
+    over_row(1)
     near(0)
     close_keys(0, b_near, (1, 0))
     close_keys(1, b_near, (1, 0))
-    spread(0)
-    project(0)
-    over_row(1)
-    for n in range(1, 6):
+    spread(1)
+    for n in range(6):
         project(n)
-    spread(1)
 
     for n, (r, got) in enumerate(((r_dq, dqr), (r_dk, dkr), (r_dv, dvr))):
         for s in range(4):

time: 84.1 us -> 84.2 us (level)
  no operation moved by 1% of the time
where the time goes in v4:
time: 84.2 us; the launch traced here: 84.1 us
  Pallas kernels  83.3 us (99%)
    pallas_call x1, Pallas kernels, on_device(): pl.pallas_call(kernel, out_shape=(jax.ShapeDtypeStruct((TILE, D), BF), *[...  79.7 us
    pallas_call x1, Pallas kernels, on_device(): pl.pallas_call(widen, out_shape=(jax.ShapeDtypeStruct((TILE, D), BF), *[j...  3.59 us

profile of v4, /device:TPU:1, one launch (start us, length us, event | category | flops | bytes accessed | tf_op | source)
XLA Modules:
  0.0 84.1 jit_solution(14528823184813778807)
XLA Ops:
  0.6 79.7 %sublayer.1 = (bf16[384,3072]{1,0:T(8,128)(2,1)}, bf16[384,512]{1,0:T(8,128)(2,1)}, bf16[384,512]{1,0:T(8,128)(2,1)}, bf16[384,512]{1,0:T(8,128)(2,1)}, bf16[64,3072]{1,0:T(8,128)(2,1)}) custom-call(bf16[384,512]{1,0:T(8,128)(2,1)} %bitcast.9, bf16[384,512]{1,0:T(8,128)(2,1)} %bitcast.10, bf16[384,512]{1,0:T(8,128)(2,1)} %bitcast.11, ...), custom_call_target="tpu_custom_call" | custom-call | tf_op jit(solution)/shard_map/sublayer/pallas_call | solution.py:545
  80.3 3.6 %widen.1 = (bf16[384,3072]{1,0:T(8,128)(2,1)}, f32[384,512]{1,0:T(8,128)}, f32[384,512]{1,0:T(8,128)}, f32[384,512]{1,0:T(8,128)}, f32[64,3072]{1,0:T(8,128)}) custom-call(bf16[384,3072]{1,0:T(8,128)(2,1)} %get-tuple-element.15.oi, bf16[384,512]{1,0:T(8,128)(2,1)} %get-tuple-element.16.qi, bf16[384,512]{1,0:T(8,128)(2,1)} %get-tuple-element.17.ki, ...), custom_call_target="tpu_custom_call" | custom-call | tf_op jit(solution)/shard_map/widen/pallas_call | solution.py:582
